TPU v7x, 256 devices: a whole 4x4x8 slice. The times are simulated.
256 devices in a mesh: comp: 32 (over x, z_lo, core), space: 8 (over z_hi, y).
Axes of the slice: x: 4, y: 4, z: 8 (z_hi: 2, z_lo: 4; z = z_hi * 4 + z_lo), core: 2. Of those that a mesh axis runs over, the one named last changes fastest.
Arguments:
- spectrum: float32 [1152, 131072], P(None, ('comp', 'space')), may hold values from 0.05 to 1
- wind_field: float32 [2, 131072], P(None, ('comp', 'space')), may hold values from -4 to 4
- coupling: bfloat16 [1152, 1152], replicated, may hold values from -0.1875 to 0.1875
- growth: float32 [32], replicated, may hold values from 0.02 to 0.2
- dissipation: float32 [32], replicated, may hold values from 0.1 to 1
- group_speed: float32 [32, 32], replicated, may hold values from 0.1 to 0.45
- refraction: float32 [32, 32], replicated, may hold values from -0.5 to 0.5
- depths: float32 [32], replicated, may hold values from 0.1 to 1
- sea_mask: int32 [1024, 128], P('space'), may hold values 0 or 1
- depth_index: int32 [1024, 128], P('space'), may hold values from 0 to 31
Outputs:
- spectrum_out: float32 [1152, 131072], P(None, ('comp', 'space'))
All inputs are finite; a program needn't handle non-finite values. No bound on the sum of `sea_mask` on one device may be relied on, other than what follows from the above.
Results may differ from a plain program's by a relative error of at most 0.00051.
Values sent between devices are 32-bit elements; how exact they have to be, the bound alone decides.
A program may use at most 64 MiB of HBM per device.

v0:
```python
import jax
import jax.numpy as jnp
from jax import lax
from jax.sharding import PartitionSpec as P

ND = 36
SUBSTEPS = 3


def extended(shard, sides, width):
    for axis, dim in sides:
        size, length = (lax.axis_size(axis), shard.shape[dim])
        up = [(i, (i + 1) % size) for i in range(size - 1)]
        down = [(j, i) for i, j in up]
        last = lax.slice_in_dim(shard, length - width, length, axis=dim)
        leading = lax.slice_in_dim(shard, 0, width, axis=dim)
        before = lax.ppermute(last, axis, up)
        after = lax.ppermute(leading, axis, down)
        shard = jnp.concatenate([before, shard, after], axis=dim)
    return shard


def direction_angles():
    return 2.0 * jnp.pi * jnp.arange(ND, dtype=jnp.float32) / ND


def source_terms(energy, wind_block, coupling, growth, dissipation):
    nfreq = growth.shape[0]
    angles = direction_angles()
    projected = (
        jnp.cos(angles)[:, None] * wind_block[0][None, :]
        + jnp.sin(angles)[:, None] * wind_block[1][None, :]
    )
    forcing = jnp.maximum(projected, 0.0)
    driving = growth[:, None, None] * (forcing * forcing)[None]
    average = jnp.mean(energy, axis=0)
    damping = dissipation[:, None, None] * (average / (average + 1.0))[None, None, :]
    nonlinear = jnp.dot(coupling, energy.astype(jnp.bfloat16), preferred_element_type=jnp.float32)
    shaped = energy.reshape(nfreq, ND, -1)
    return (shaped + (driving - damping) * shaped).reshape(energy.shape) + 0.25 * nonlinear


def face_flux(behind, centre, forward, beyond, courant):
    central = 0.5 * (centre + forward) - 0.5 * courant * (forward - centre)
    curvature = jnp.where(
        courant >= 0.0, forward - 2.0 * centre + behind, beyond - 2.0 * forward + centre
    )
    return courant * (central - (1.0 - courant * courant) / 6.0 * curvature)


def cut_along(values, offset, length, along):
    return lax.slice_in_dim(values, offset, offset + length, axis=along)


def advect(padded, speeds, weight, along):
    inner_count = padded.shape[along] - 4
    courant = 0.5 * (
        cut_along(speeds, 1, inner_count + 1, along) + cut_along(speeds, 2, inner_count + 1, along)
    )
    if weight is not None:
        courant = (
            courant
            * cut_along(weight, 1, inner_count + 1, along)
            * cut_along(weight, 2, inner_count + 1, along)
        )
    face_values = face_flux(
        cut_along(padded, 0, inner_count + 1, along),
        cut_along(padded, 1, inner_count + 1, along),
        cut_along(padded, 2, inner_count + 1, along),
        cut_along(padded, 3, inner_count + 1, along),
        courant,
    )
    return cut_along(padded, 2, inner_count, along) - (
        cut_along(face_values, 1, inner_count, along)
        - cut_along(face_values, 0, inner_count, along)
    )


def pad_zero(values, along, width):
    padding = [(0, 0)] * values.ndim
    padding[along] = (width, width)
    return jnp.pad(values, padding)


def wrap_dirs(values, along):
    length = values.shape[along]
    return jnp.concatenate(
        [cut_along(values, length - 2, 2, along), values, cut_along(values, 0, 2, along)],
        axis=along,
    )


def surface_slopes(height):
    rows_padded = jnp.pad(height, ((1, 1), (0, 0)))
    cols_padded = jnp.pad(height, ((0, 0), (1, 1)))
    return (
        0.5 * (rows_padded[2:] - rows_padded[:-2]),
        0.5 * (cols_padded[:, 2:] - cols_padded[:, :-2]),
    )


def transport_speeds(speed_pts, refract_pts, height):
    angles = direction_angles()
    cosine_dir = jnp.cos(angles)[:, None, None]
    sine_dir = jnp.sin(angles)[:, None, None]
    slope_x, slope_y = surface_slopes(height)
    speed_wide = jnp.expand_dims(speed_pts, -3)
    speed_x = speed_wide * cosine_dir
    speed_y = speed_wide * sine_dir
    speed_dir = jnp.expand_dims(refract_pts, -3) * (sine_dir * slope_x - cosine_dir * slope_y)
    return (speed_x, speed_y, speed_dir)


def cross_passes(energy, speed_y, speed_dir, mask_wide):
    y_axis = energy.ndim - 1
    dir_axis = energy.ndim - 3
    energy = advect(
        pad_zero(energy, y_axis, 2),
        pad_zero(speed_y, y_axis, 2),
        pad_zero(mask_wide, y_axis, 2),
        y_axis,
    )
    energy = advect(wrap_dirs(energy, dir_axis), wrap_dirs(speed_dir, dir_axis), None, dir_axis)
    return energy * mask_wide


def per_device(
    spectrum,
    wind_field,
    coupling,
    growth,
    dissipation,
    group_speed,
    refraction,
    depths,
    sea_mask,
    depth_index,
):
    comp_count = lax.axis_size("comp")
    components = spectrum.shape[0]
    group_size = components // comp_count
    nfreq_local = group_size // ND
    strip_rows = sea_mask.shape[0]
    width_y = sea_mask.shape[1]
    regrouped = lax.all_to_all(
        source_terms(spectrum, wind_field, coupling, growth, dissipation),
        "comp",
        split_axis=0,
        concat_axis=1,
        tiled=True,
    )
    energy = regrouped.reshape(nfreq_local, ND, strip_rows, width_y)
    margin = 2
    coast_cells = extended(jnp.stack([sea_mask, depth_index]), (("space", 1),), margin)
    mask_ext = coast_cells[0].astype(jnp.float32)
    levels = depths.shape[0]
    onehot = (coast_cells[1].reshape(1, -1) == jnp.arange(levels, dtype=jnp.int32)[:, None]).astype(
        jnp.float32
    )
    first_freq = lax.axis_index("comp") * nfreq_local
    tables = jnp.concatenate(
        [
            depths[None, :],
            lax.dynamic_slice_in_dim(group_speed, first_freq, nfreq_local, 0),
            lax.dynamic_slice_in_dim(refraction, first_freq, nfreq_local, 0),
        ],
        axis=0,
    )
    looked = jnp.dot(tables, onehot, precision=lax.Precision.HIGHEST).reshape(
        1 + 2 * nfreq_local, strip_rows + 2 * margin, width_y
    )
    height = looked[0] * mask_ext
    speed_x, speed_y, speed_dir = transport_speeds(
        looked[1 : 1 + nfreq_local], looked[1 + nfreq_local :], height
    )
    mask_wide = mask_ext[None, None]
    for substep in range(SUBSTEPS):
        padded = extended(energy, (("space", 2),), 2)
        energy = advect(padded, speed_x, mask_wide, 2)
        energy = cross_passes(
            energy, speed_y[:, :, 2:-2], speed_dir[:, :, 2:-2], mask_wide[:, :, 2:-2]
        )
    flattened = energy.reshape(group_size, strip_rows * width_y)
    return lax.all_to_all(flattened, "comp", split_axis=1, concat_axis=0, tiled=True)


def solution(mesh):
    in_specs = (
        P(None, ("comp", "space")),
        P(None, ("comp", "space")),
        P(),
        P(),
        P(),
        P(),
        P(),
        P(),
        P("space", None),
        P("space", None),
    )
    out_specs = P(None, ("comp", "space"))
    return jax.shard_map(
        per_device, mesh=mesh, in_specs=in_specs, out_specs=out_specs, check_vma=False
    )
```

profile of v0, /device:TPU:24, one launch (start us, length us, event | category | flops | bytes accessed | tf_op | source)
XLA Modules:
  0.0 256.0 jit_solution(8397670580517595374)
XLA Ops:
  0.0 0.9 fusion.114
  1.0 1.8 mul.517
  2.8 3.4 %mul.518 = f32[1152,512]{1,0:T(8,128)} reshape(f32[32,36,512]{2,1,0:T(8,128)} %mul.517) | data formatting | bytes 4718592 | tf_op jit(solution)/shard_map/mul | solution.py:35
  6.2 1.9 reduce_sum.9
  8.2 1.8 sub.231
  10.0 3.4 %sub.232 = f32[1152,512]{1,0:T(8,128)} reshape(f32[32,36,512]{2,1,0:T(8,128)} %sub.231) | data formatting | bytes 4718592 | tf_op jit(solution)/shard_map/sub | solution.py:40
  13.6 7.0 %fusion.24 = f32[1152,512]{1,0:T(8,128)} fusion(bf16[1152,1152]{1,0:T(8,128)(2,1)S(1)} %copy-done, f32[1152,512]{1,0:T(8,128)} %param.10, f32[1152,512]{1,0:T(8,128)} %sub.232, f32[1152,512]{1,0:T(8,128)} %mul.518, f32[1152]{0:T(1024)S(1)} %mul.508), kind=kOutput, calls=%fused_computation.41 | convolution fusion | flops 1363083264 | bytes 12096000 | tf_op jit(solution)/shard_map/dot_general | solution.py:38
  20.7 3.3 %all_to_all.26 = f32[32,36,512]{2,1,0:T(8,128)} reshape(f32[1152,512]{1,0:T(8,128)} %fusion.24) | data formatting | bytes 4718592 | tf_op jit(solution)/shard_map/all_to_all | solution.py:145
  24.0 8.9 %all-to-all-start = ((f32[32,36,512]{2,1,0:T(8,128)}), f32[32,36,512]{2,1,0:T(8,128)S(1)}, u32[]{:S(2)}, u32[]{:S(2)}) async-start(f32[32,36,512]{2,1,0:T(8,128)} %all_to_all.26), calls=%async_computation | async-start | bytes 5242880 | tf_op jit(solution)/shard_map/all_to_all | solution.py:145
  32.9 6.1 %collective-permute-start = (s32[2,2,128]{2,1,0:T(2,128)S(1)}, s32[2,2,128]{2,1,0:T(2,128)S(1)}, u32[]{:S(2)}, u32[]{:S(2)}) collective-permute-start(s32[2,2,128]{2,1,0:T(2,128)S(1)} %get-tuple-element.28), channel_id=1, source_target_pairs={{0,1},{1,2},{2,3},{3,4},{4,5},{5,6},{6,7},{8,9},{9,10},{10,11},{11... | collective-permute-start | bytes 6152 | tf_op jit(solution)/shard_map/ppermute | solution.py:17
  39.0 1.9 collective-permute-start.1
  40.9 0.7 constant_dynamic-slice_fusion
  41.6 34.5 %collective-permute-done = s32[2,2,128]{2,1,0:T(2,128)S(1)} collective-permute-done((s32[2,2,128]{2,1,0:T(2,128)S(1)}, s32[2,2,128]{2,1,0:T(2,128)S(1)}, u32[]{:S(2)}, u32[]{:S(2)}) %collective-permute-start) | collective-permute-done | bytes 2080 | tf_op jit(solution)/shard_map/ppermute | solution.py:17
  76.1 4.5 %collective-permute-done.1 = s32[2,2,128]{2,1,0:T(2,128)S(1)} collective-permute-done((s32[2,2,128]{2,1,0:T(2,128)S(1)}, s32[2,2,128]{2,1,0:T(2,128)S(1)}, u32[]{:S(2)}, u32[]{:S(2)}) %collective-permute-start.1) | collective-permute-done | bytes 2080 | tf_op jit(solution)/shard_map/ppermute | solution.py:18
  80.7 0.8 fusion.87
  82.1 2.1 subtract_multiply_fusion.1
  84.2 1.7 slice.468
  86.1 1.7 broadcast_multiply_fusion.1
  87.8 6.8 %all-to-all-done = f32[32,36,512]{2,1,0:T(8,128)S(1)} async-done(((f32[32,36,512]{2,1,0:T(8,128)}), f32[32,36,512]{2,1,0:T(8,128)S(1)}, u32[]{:S(2)}, u32[]{:S(2)}) %all-to-all-start) | async-done | bytes 2359328 | tf_op jit(solution)/shard_map/all_to_all | solution.py:145
  94.6 2.8 %copy.13 = f32[36,32,512]{2,1,0:T(8,128)} copy(f32[36,32,512]{2,0,1:T(8,128)S(1)} %bitcast.30) | data formatting | bytes 4718592 | tf_op jit(solution)/shard_map/all_to_all | solution.py:145
  97.4 2.3 reshape.204
  99.8 2.7 %collective-permute-start.3 = (f32[1,36,2,128]{3,2,1,0:T(2,128)S(1)}, f32[1,36,2,128]{3,2,1,0:T(2,128)S(1)}, u32[]{:S(2)}, u32[]{:S(2)}) collective-permute-start(f32[1,36,2,128]{3,2,1,0:T(2,128)S(1)} %get-tuple-element.25), channel_id=1, source_target_pairs={{1,0},{2,1},{3,2},{4,3},{5,4},{6,5},{7,6},{9,8},{10,9},{11,10},{12... | collective-permute-start | bytes 110600 | tf_op jit(solution)/shard_map/ppermute | solution.py:18
  102.7 9.4 %collective-permute-start.2 = (f32[1,36,2,128]{3,2,1,0:T(2,128)S(1)}, f32[1,36,2,128]{3,2,1,0:T(2,128)S(1)}, u32[]{:S(2)}, u32[]{:S(2)}) collective-permute-start(f32[1,36,2,128]{3,2,1,0:T(2,128)S(1)} %get-tuple-element.24), channel_id=1, source_target_pairs={{0,1},{1,2},{2,3},{3,4},{4,5},{5,6},{6,7},{8,9},{9,10},{10,11},{11... | collective-permute-start | bytes 110600 | tf_op jit(solution)/shard_map/ppermute | solution.py:17
  112.2 1.4 collective-permute-done.2
  113.6 2.8 %fusion.43 = (f32[1,36,129,128]{3,2,1,0:T(8,128)S(1)}, f32[1,36,129,128]{3,2,1,0:T(8,128)S(1)}) fusion(f32[1,36,130,128]{3,2,1,0:T(8,128)S(1)} %constant_dynamic-update-slice_fusion, f32[1,36,128,128]{3,2,1,0:T(8,128)S(1)} %reshape.204, f32[1,36,2,128]{3,2,1,0:T(2,128)S(1)} %collective-permute-done.2, f32[129,128]{1,0:T(8,128)S(1)} %get-tuple-element.35, ...), kind=kLoop, calls=%fused_computation.69 | loop fusion | flops 14860800 | bytes 16794624 | tf_op jit(solution)/shard_map/mul | solution.py:48
  116.8 1.3 copy-done.4
  118.1 4.9 %fusion.7 = (f32[1,36,128,129]{3,2,1,0:T(8,128)S(1)}, f32[1,36,128,129]{3,2,1,0:T(8,128)S(1)}) fusion(f32[1,36,128,128]{3,2,1,0:T(8,128)S(1)} %fusion.86, f32[128,129]{1,0:T(8,128)S(1)} %get-tuple-element.37, f32[128,129]{1,0:T(8,128)S(1)} %get-tuple-element.36, f32[1,36,128,128]{3,2,1,0:T(8,128)S(1)} %copy-done.4), kind=kLoop, calls=%fused_computation.21 | loop fusion | flops 13671936 | bytes 9606144 | tf_op jit(solution)/shard_map/mul | solution.py:48
  123.0 0.7 fusion.85
  123.7 0.9 copy-done.2
  124.6 1.8 fusion.72
  126.9 10.2 %collective-permute-start.4 = (f32[1,36,2,128]{3,2,1,0:T(2,128)S(1)}, f32[1,36,2,128]{3,2,1,0:T(2,128)S(1)}, u32[]{:S(2)}, u32[]{:S(2)}) collective-permute-start(f32[1,36,2,128]{3,2,1,0:T(2,128)S(1)} %get-tuple-element.20), channel_id=1, source_target_pairs={{0,1},{1,2},{2,3},{3,4},{4,5},{5,6},{6,7},{8,9},{9,10},{10,11},{11... | collective-permute-start | bytes 110600 | tf_op jit(solution)/shard_map/ppermute | solution.py:17
  137.2 1.9 collective-permute-start.5
  139.1 9.9 %collective-permute-done.5 = f32[1,36,2,128]{3,2,1,0:T(2,128)S(1)} collective-permute-done((f32[1,36,2,128]{3,2,1,0:T(2,128)S(1)}, f32[1,36,2,128]{3,2,1,0:T(2,128)S(1)}, u32[]{:S(2)}, u32[]{:S(2)}) %collective-permute-start.5) | collective-permute-done | bytes 36896 | tf_op jit(solution)/shard_map/ppermute | solution.py:18
  149.1 2.3 fusion.37
  151.7 3.6 %fusion.14 = f32[1,36,128,129]{3,2,1,0:T(8,128)S(1)} fusion(f32[1,36,128,129]{3,2,1,0:T(8,128)S(1)} %get-tuple-element.9, f32[1,36,128,128]{3,2,1,0:T(8,128)S(1)} %fusion.82), kind=kLoop, calls=%fused_computation.28 | loop fusion | flops 11888640 | bytes 7114752 | tf_op jit(solution)/shard_map/mul | solution.py:48
  156.1 1.8 fusion.65
  158.4 1.9 collective-permute-start.6
  160.3 4.1 %collective-permute-start.7 = (f32[1,36,2,128]{3,2,1,0:T(2,128)S(1)}, f32[1,36,2,128]{3,2,1,0:T(2,128)S(1)}, u32[]{:S(2)}, u32[]{:S(2)}) collective-permute-start(f32[1,36,2,128]{3,2,1,0:T(2,128)S(1)} %get-tuple-element.17), channel_id=1, source_target_pairs={{1,0},{2,1},{3,2},{4,3},{5,4},{6,5},{7,6},{9,8},{10,9},{11,10},{12... | collective-permute-start | bytes 110600 | tf_op jit(solution)/shard_map/ppermute | solution.py:18
  164.5 7.7 %collective-permute-done.7 = f32[1,36,2,128]{3,2,1,0:T(2,128)S(1)} collective-permute-done((f32[1,36,2,128]{3,2,1,0:T(2,128)S(1)}, f32[1,36,2,128]{3,2,1,0:T(2,128)S(1)}, u32[]{:S(2)}, u32[]{:S(2)}) %collective-permute-start.7) | collective-permute-done | bytes 36896 | tf_op jit(solution)/shard_map/ppermute | solution.py:18
  172.2 2.3 fusion.30
  174.9 3.6 %fusion.21 = f32[1,36,128,129]{3,2,1,0:T(8,128)S(1)} fusion(f32[1,36,128,129]{3,2,1,0:T(8,128)S(1)} %get-tuple-element.9, f32[1,36,128,128]{3,2,1,0:T(8,128)S(1)} %fusion.78), kind=kLoop, calls=%fused_computation.35 | loop fusion | flops 11888640 | bytes 7114752 | tf_op jit(solution)/shard_map/mul | solution.py:48
  178.5 0.7 fusion.77
  179.2 2.0 fusion.58
  181.3 1.8 fusion.76
  183.1 2.4 all_to_all.29
  185.6 1.4 copy.14
  187.0 65.6 %all_to_all.35 = f32[36,32,512]{2,0,1:T(8,128)} all-to-all(f32[36,32,512]{2,0,1:T(8,128)S(1)} %copy.14), channel_id=1, replica_groups=mesh['comp'=32,'space'=8] {'comp'}, dimensions={1} | all-to-all | bytes 4718592 | tf_op jit(solution)/shard_map/all_to_all | solution.py:184
  252.6 3.4 %all_to_all.32 = f32[1152,512]{1,0:T(8,128)} reshape(f32[32,36,512]{2,1,0:T(8,128)} %bitcast.31) | data formatting | bytes 4718592 | tf_op jit(solution)/shard_map/all_to_all | solution.py:184
  (52 shorter events, 4.3 us)
Async XLA Ops:
  0.0 13.6 %copy-start = (bf16[1152,1152]{1,0:T(8,128)(2,1)S(1)}, bf16[1152,1152]{1,0:T(8,128)(2,1)}, u32[]{:S(2)}) copy-start(bf16[1152,1152]{1,0:T(8,128)(2,1)} %param.12) | copy-start | bytes 7962628
  2.8 5.3 %copy-start.7 = (f32[32]{0:T(128)S(1)}, f32[32]{0:T(128)}, u32[]{:S(2)}) copy-start(f32[32]{0:T(128)} %param.14) | copy-start | bytes 388
  10.0 3.4 %copy-start.8 = (f32[32]{0:T(128)S(1)}, f32[32]{0:T(128)}, u32[]{:S(2)}) copy-start(f32[32]{0:T(128)} %param.13) | copy-start | bytes 388
  24.0 8.9 %copy-start.5 = (s32[128,128]{1,0:T(8,128)S(1)}, s32[128,128]{1,0:T(8,128)}, u32[]{:S(2)}) copy-start(s32[128,128]{1,0:T(8,128)} %param.19) | copy-start | bytes 196612
  24.0 8.9 %copy-start.6 = (s32[128,128]{1,0:T(8,128)S(1)}, s32[128,128]{1,0:T(8,128)}, u32[]{:S(2)}) copy-start(s32[128,128]{1,0:T(8,128)} %param.18) | copy-start | bytes 196612
  24.0 56.7 %copy-start.9 = (f32[32]{0:T(128)S(1)}, f32[32]{0:T(128)}, u32[]{:S(2)}) copy-start(f32[32]{0:T(128)} %param.17) | copy-start | bytes 388
  24.0 70.6 %all-to-all-start = ((f32[32,36,512]{2,1,0:T(8,128)}), f32[32,36,512]{2,1,0:T(8,128)S(1)}, u32[]{:S(2)}, u32[]{:S(2)}) async-start(f32[32,36,512]{2,1,0:T(8,128)} %all_to_all.26), calls=%async_computation | async-start | bytes 5242880 | tf_op jit(solution)/shard_map/all_to_all | solution.py:145
  32.9 43.2 %collective-permute-start = (s32[2,2,128]{2,1,0:T(2,128)S(1)}, s32[2,2,128]{2,1,0:T(2,128)S(1)}, u32[]{:S(2)}, u32[]{:S(2)}) collective-permute-start(s32[2,2,128]{2,1,0:T(2,128)S(1)} %get-tuple-element.28), channel_id=1, source_target_pairs={{0,1},{1,2},{2,3},{3,4},{4,5},{5,6},{6,7},{8,9},{9,10},{10,11},{11... | collective-permute-start | bytes 6152 | tf_op jit(solution)/shard_map/ppermute | solution.py:17
  39.0 41.7 %collective-permute-start.1 = (s32[2,2,128]{2,1,0:T(2,128)S(1)}, s32[2,2,128]{2,1,0:T(2,128)S(1)}, u32[]{:S(2)}, u32[]{:S(2)}) collective-permute-start(s32[2,2,128]{2,1,0:T(2,128)S(1)} %get-tuple-element.29), channel_id=1, source_target_pairs={{1,0},{2,1},{3,2},{4,3},{5,4},{6,5},{7,6},{9,8},{10,9},{11,10},{12... | collective-permute-start | bytes 6152 | tf_op jit(solution)/shard_map/ppermute | solution.py:18
  99.8 13.8 %copy-start.3 = (f32[1,36,132,128]{3,2,1,0:T(8,128)S(1)}, f32[1,36,132,128]{3,2,1,0:T(8,128)}, u32[]{:S(2)}) copy-start(f32[1,36,132,128]{3,2,1,0:T(8,128)} %get-tuple-element.41) | copy-start | bytes 7299076
  99.8 12.4 %collective-permute-start.3 = (f32[1,36,2,128]{3,2,1,0:T(2,128)S(1)}, f32[1,36,2,128]{3,2,1,0:T(2,128)S(1)}, u32[]{:S(2)}, u32[]{:S(2)}) collective-permute-start(f32[1,36,2,128]{3,2,1,0:T(2,128)S(1)} %get-tuple-element.25), channel_id=1, source_target_pairs={{1,0},{2,1},{3,2},{4,3},{5,4},{6,5},{7,6},{9,8},{10,9},{11,10},{12... | collective-permute-start | bytes 110600 | tf_op jit(solution)/shard_map/ppermute | solution.py:18
  102.7 10.9 %collective-permute-start.2 = (f32[1,36,2,128]{3,2,1,0:T(2,128)S(1)}, f32[1,36,2,128]{3,2,1,0:T(2,128)S(1)}, u32[]{:S(2)}, u32[]{:S(2)}) collective-permute-start(f32[1,36,2,128]{3,2,1,0:T(2,128)S(1)} %get-tuple-element.24), channel_id=1, source_target_pairs={{0,1},{1,2},{2,3},{3,4},{4,5},{5,6},{6,7},{8,9},{9,10},{10,11},{11... | collective-permute-start | bytes 110600 | tf_op jit(solution)/shard_map/ppermute | solution.py:17
  116.4 1.7 copy-start.4
  123.0 1.7 copy-start.2
  126.9 12.2 %collective-permute-start.4 = (f32[1,36,2,128]{3,2,1,0:T(2,128)S(1)}, f32[1,36,2,128]{3,2,1,0:T(2,128)S(1)}, u32[]{:S(2)}, u32[]{:S(2)}) collective-permute-start(f32[1,36,2,128]{3,2,1,0:T(2,128)S(1)} %get-tuple-element.20), channel_id=1, source_target_pairs={{0,1},{1,2},{2,3},{3,4},{4,5},{5,6},{6,7},{8,9},{9,10},{10,11},{11... | collective-permute-start | bytes 110600 | tf_op jit(solution)/shard_map/ppermute | solution.py:17
  137.2 11.9 %collective-permute-start.5 = (f32[1,36,2,128]{3,2,1,0:T(2,128)S(1)}, f32[1,36,2,128]{3,2,1,0:T(2,128)S(1)}, u32[]{:S(2)}, u32[]{:S(2)}) collective-permute-start(f32[1,36,2,128]{3,2,1,0:T(2,128)S(1)} %get-tuple-element.21), channel_id=1, source_target_pairs={{1,0},{2,1},{3,2},{4,3},{5,4},{6,5},{7,6},{9,8},{10,9},{11,10},{12... | collective-permute-start | bytes 110600 | tf_op jit(solution)/shard_map/ppermute | solution.py:18
  158.4 6.1 %collective-permute-start.6 = (f32[1,36,2,128]{3,2,1,0:T(2,128)S(1)}, f32[1,36,2,128]{3,2,1,0:T(2,128)S(1)}, u32[]{:S(2)}, u32[]{:S(2)}) collective-permute-start(f32[1,36,2,128]{3,2,1,0:T(2,128)S(1)} %get-tuple-element.16), channel_id=1, source_target_pairs={{0,1},{1,2},{2,3},{3,4},{4,5},{5,6},{6,7},{8,9},{9,10},{10,11},{11... | collective-permute-start | bytes 110600 | tf_op jit(solution)/shard_map/ppermute | solution.py:17
  160.3 11.9 %collective-permute-start.7 = (f32[1,36,2,128]{3,2,1,0:T(2,128)S(1)}, f32[1,36,2,128]{3,2,1,0:T(2,128)S(1)}, u32[]{:S(2)}, u32[]{:S(2)}) collective-permute-start(f32[1,36,2,128]{3,2,1,0:T(2,128)S(1)} %get-tuple-element.17), channel_id=1, source_target_pairs={{1,0},{2,1},{3,2},{4,3},{5,4},{6,5},{7,6},{9,8},{10,9},{11,10},{12... | collective-permute-start | bytes 110600 | tf_op jit(solution)/shard_map/ppermute | solution.py:18
  186.9 69.0 %copy-start.1 = (bf16[1152,1152]{1,0:T(8,128)(2,1)S(1)}, bf16[1152,1152]{1,0:T(8,128)(2,1)}, u32[]{:S(2)}) copy-start(bf16[1152,1152]{1,0:T(8,128)(2,1)} %param.12) | copy-start | bytes 7962628
where the time goes:
time: 257 us; the launch traced here: 256 us
  blocking collectives  65.6 us (26%)
  waiting for transfers between devices  64.9 us (25%)
  starting transfers between devices  47.3 us (18%)
  other arithmetic  37.2 us (14%)
  local copies, waits for them, and re-layouts  32.7 us (13%)
  matrix products  7.77 us (3%)
    all_to_all x1, blocking collectives, per_device(): lax.all_to_all(flattened, 'comp', split_axis=1, concat_axis=0, tiled=True)  65.6 us
    ppermute x4, waiting for transfers between devices, extended(): before = lax.ppermute(last, axis, up)  35.9 us
    ppermute x4, starting transfers between devices, extended(): before = lax.ppermute(last, axis, up)  27.7 us
    mul x9, other arithmetic, face_flux(): return courant * (central - (1.0 - courant * courant) / 6.0 * curvature)  25.1 us
    ppermute x4, waiting for transfers between devices, extended(): after = lax.ppermute(leading, axis, down)  22.2 us
    ppermute x4, starting transfers between devices, extended(): after = lax.ppermute(leading, axis, down)  10.7 us
    all_to_all x1, starting transfers between devices, per_device(): lax.all_to_all(source_terms(spectrum, wind_field, coupling, growth, dissi...  8.89 us
    all_to_all x3, local copies, waits for them, and re-layouts, per_device(): lax.all_to_all(flattened, 'comp', split_axis=1, concat_axis=0, tiled=True)  7.22 us
  transfers between devices with their start and end apart: 9, of which 6 were waited for; matrix products, arithmetic and copies ran while one was open for 3% of the time, Pallas kernels for 0%

commit v1 on v0

v1 whole, which is shorter than its diff:
```python
import functools

import jax
import jax.numpy as jnp
import numpy as np
from jax import lax
from jax.experimental import pallas as pl
from jax.experimental.pallas import tpu as pltpu
from jax.sharding import PartitionSpec as P

ND = 36
NQ = 9
RB = 4
NY = 128
SUBSTEPS = 3
FB = 8
SLOTS = 6 * NQ
MESH = pl.DeviceIdType.MESH


def direction_tables():
    angles = np.float32(2.0 * np.pi) * np.arange(ND, dtype=np.float32) / np.float32(ND)
    cosine = np.cos(angles.astype(np.float64)).astype(np.float32)
    sine = np.sin(angles.astype(np.float64)).astype(np.float32)
    half_cos = np.float32(0.5) * (cosine + np.roll(cosine, -1))
    half_sin = np.float32(0.5) * (sine + np.roll(sine, -1))
    return np.concatenate([cosine, sine, half_cos, half_sin])


def face_of(nu, base, diff, second):
    return nu * (base + (1.0 - nu) * (0.5 * diff - (nu * (1.0 / 6.0) + (1.0 / 6.0)) * second))


def kernel(
    nfreq,
    ncomp,
    nspace,
    trig,
    growth,
    dissipation,
    depths,
    wind,
    group_speed,
    refraction,
    sea_mask,
    depth_index,
    spectrum,
    coupling,
    out,
    spec_v,
    coup_v,
    spec_b,
    nonlin,
    energy,
    work,
    out_v,
    send_l,
    send_r,
    recv_l,
    recv_r,
    coast_out,
    coast_in,
    gx,
    gy,
    rx,
    ry,
    mask_v,
    wind_v,
    ratio_v,
    load_sem,
    coup_sem,
    store_sem,
    send_l_sem,
    send_r_sem,
    recv_l_sem,
    recv_r_sem,
    coast_send_sem,
    coast_recv_sem,
):
    blocks = nfreq // FB
    rows_b = FB * ND
    components = nfreq * ND
    c = lax.axis_index("comp")
    s = lax.axis_index("space")
    total = ncomp * nspace
    n = s * ncomp + c
    before = lax.rem(n + total - 1, total)
    after = lax.rem(n + 1, total)
    left = (lax.rem(before, ncomp), lax.div(before, ncomp))
    right = (lax.rem(after, ncomp), lax.div(after, ncomp))
    edge_l = jnp.where(n > 0, 1.0, 0.0).astype(jnp.float32)
    edge_r = jnp.where(n < total - 1, 1.0, 0.0).astype(jnp.float32)

    barrier = pltpu.get_barrier_semaphore()
    pl.semaphore_signal(barrier, inc=1, device_id=left, device_id_type=MESH)
    pl.semaphore_signal(barrier, inc=1, device_id=right, device_id_type=MESH)

    def lanes(r):
        return slice(r * NY, (r + 1) * NY)

    def spec_load(r):
        return pltpu.make_async_copy(spectrum.at[:, lanes(r)], spec_v.at[r], load_sem.at[r])

    for r in range(RB):
        spec_load(r).start()

    def coup_load(b):
        rows = pl.ds(pl.multiple_of(b * rows_b, rows_b), rows_b)
        return pltpu.make_async_copy(coupling.at[rows], coup_v.at[rows], coup_sem.at[b])

    for b in range(blocks):
        coup_load(b).start()

    own_mask = [sea_mask[pl.ds(c * RB + r, 1), :] for r in range(RB)]
    own_index = [depth_index[pl.ds(c * RB + r, 1), :] for r in range(RB)]
    for side, r in ((0, 0), (1, RB - 1)):
        coast_out[side, 0] = jnp.broadcast_to(own_mask[r], (8, NY))
        coast_out[side, 1] = jnp.broadcast_to(own_index[r], (8, NY))

    pl.semaphore_wait(barrier, 2)

    def coast_copy(side):
        return pltpu.make_async_remote_copy(
            src_ref=coast_out.at[side],
            dst_ref=coast_in.at[1 - side],
            send_sem=coast_send_sem.at[side],
            recv_sem=coast_recv_sem.at[1 - side],
            device_id=left if side == 0 else right,
            device_id_type=MESH,
        )

    for side in range(2):
        coast_copy(side).start()

    def to_left(k):
        return pltpu.make_async_remote_copy(
            src_ref=send_l.at[k],
            dst_ref=recv_r.at[k],
            send_sem=send_l_sem.at[k],
            recv_sem=recv_r_sem.at[k],
            device_id=left,
            device_id_type=MESH,
        )

    def to_right(k):
        return pltpu.make_async_remote_copy(
            src_ref=send_r.at[k],
            dst_ref=recv_l.at[k],
            send_sem=send_r_sem.at[k],
            recv_sem=recv_l_sem.at[k],
            device_id=right,
            device_id_type=MESH,
        )

    for r in range(RB):
        spec_load(r).wait()

        def cast_rows(i, acc, r=r):
            rows = pl.ds(pl.multiple_of(i * 64, 64), 64)
            block = spec_v[r, rows, :]
            spec_b[rows, lanes(r)] = block.astype(jnp.bfloat16)
            return acc + jnp.sum(block.reshape(8, 8, NY), axis=0)

        acc = lax.fori_loop(0, components // 64, cast_rows, jnp.zeros((8, NY), jnp.float32))
        average = jnp.sum(acc, axis=0, keepdims=True) * (1.0 / components)
        ratio_v[:, lanes(r)] = jnp.broadcast_to(average / (average + 1.0), (8, NY))
    wind_v[0] = jnp.broadcast_to(wind[0:1, :], (8, RB * NY))
    wind_v[1] = jnp.broadcast_to(wind[1:2, :], (8, RB * NY))

    for side in range(2):
        coast_copy(side).wait()
    mask_rows = (
        [coast_in[0, 0, 0:1, :].astype(jnp.float32) * edge_l]
        + [m.astype(jnp.float32) for m in own_mask]
        + [coast_in[1, 0, 0:1, :].astype(jnp.float32) * edge_r]
    )
    index_rows = [coast_in[0, 1, 0:1, :]] + own_index + [coast_in[1, 1, 0:1, :]]
    levels = depths.shape[0]
    level = lax.broadcasted_iota(jnp.int32, (levels, NY), 0)
    onehot = jnp.concatenate(
        [(jnp.broadcast_to(row, (levels, NY)) == level).astype(jnp.float32) for row in index_rows], axis=1
    )
    speeds = jnp.dot(
        group_speed[...], onehot, precision=lax.Precision.HIGHEST, preferred_element_type=jnp.float32
    )
    turning = jnp.dot(
        refraction[...],
        onehot[:, NY : (RB + 1) * NY],
        precision=lax.Precision.HIGHEST,
        preferred_element_type=jnp.float32,
    )
    lane_row = lax.broadcasted_iota(jnp.int32, (1, NY), 1)
    heights = []
    for row, mask in zip(index_rows, mask_rows):
        height = jnp.zeros((1, NY), jnp.float32)
        for entry in range(levels):
            height = jnp.where(row == entry, depths[entry], height)
        heights.append(height * mask)
    for j in range(RB + 1):
        pair = 0.5 * (speeds[:, lanes(j)] + speeds[:, lanes(j + 1)])
        gx[j] = pair * (mask_rows[j] * mask_rows[j + 1])
    for r in range(RB):
        mask = mask_rows[r + 1]
        own = speeds[:, lanes(r + 1)]
        beyond = jnp.where(lane_row == NY - 1, 0.0, pltpu.roll(jnp.broadcast_to(mask, (8, NY)), NY - 1, 1)[:1])
        gy[r] = 0.5 * (own + pltpu.roll(own, NY - 1, 1)) * (mask * beyond)
        wide = jnp.broadcast_to(heights[r + 1], (8, NY))
        up = jnp.where(lane_row == NY - 1, 0.0, pltpu.roll(wide, NY - 1, 1)[:1])
        down = jnp.where(lane_row == 0, 0.0, pltpu.roll(wide, 1, 1)[:1])
        rx[r] = turning[:, lanes(r)] * (0.5 * (heights[r + 2] - heights[r]))
        ry[r] = turning[:, lanes(r)] * (0.5 * (up - down))
        mask_v[r] = jnp.broadcast_to(mask, (8, NY))

    def pack(q, i, k, rows):
        if q in (0, 3):
            at = i + (0 if q == 0 else NQ)
            send_r[k, 2 * at] = rows[RB - 2]
            send_r[k, 2 * at + 1] = rows[RB - 1]
            send_l[k, 4 * NQ + at] = rows[0]
        else:
            at = i + (0 if q == 1 else NQ)
            send_l[k, 2 * at] = rows[0]
            send_l[k, 2 * at + 1] = rows[1]
            send_r[k, 4 * NQ + at] = rows[RB - 1]

    sub8 = lax.broadcasted_iota(jnp.int32, (FB, NY), 0)

    def by_freq(table, b):
        values = jnp.zeros((FB, NY), jnp.float32)
        for j in range(FB):
            values = jnp.where(sub8 == j, table[b * FB + j], values)
        return values

    def source(b, carry):
        coup_load(b).wait()
        rows = pl.ds(pl.multiple_of(b * rows_b, rows_b), rows_b)
        product = jnp.dot(coup_v[rows, :], spec_b[...], preferred_element_type=jnp.float32)
        for r in range(RB):
            nonlin[r] = product[:, lanes(r)]
        grow = by_freq(growth, b)
        damp = by_freq(dissipation, b)
        damps = [damp * ratio_v[:, lanes(r)] for r in range(RB)]

        def directions(i, inner):
            for q in range(4):
                d = q * NQ + i
                cosine = trig[d]
                sine = trig[ND + d]
                made = []
                for r in range(RB):
                    forcing = jnp.maximum(cosine * wind_v[0, :, lanes(r)] + sine * wind_v[1, :, lanes(r)], 0.0)
                    value = spec_v[r, pl.ds(b * rows_b + d, FB, stride=ND), :]
                    extra = nonlin[r, pl.ds(d, FB, stride=ND), :]
                    value = value + (grow * (forcing * forcing) - damps[r]) * value + 0.25 * extra
                    energy[b, d, r] = value
                    made.append(value)
                pack(q, i, b, made)
            return inner

        lax.fori_loop(0, NQ, directions, 0)
        to_left(b).start()
        to_right(b).start()
        return carry

    lax.fori_loop(0, blocks, source, 0)

    lane8 = lax.broadcasted_iota(jnp.int32, (FB, NY), 1)
    first_lane = lane8 == 0
    last_lane = lane8 == NY - 1

    def passes(k, b, emit):
        to_left(k).wait_recv()
        to_right(k).wait_recv()
        freqs = pl.ds(pl.multiple_of(b * FB, FB), FB)

        def along_x_and_y(i, carry):
            for q in range(4):
                d = q * NQ + i
                cosine = trig[d]
                sine = trig[ND + d]
                own = [energy[b, d, r] for r in range(RB)]
                at = i + (0 if q in (0, 1) else NQ)
                if q in (0, 3):
                    ext = [recv_l[k, 2 * at] * edge_l, recv_l[k, 2 * at + 1] * edge_l]
                    ext = ext + own + [recv_r[k, 4 * NQ + at] * edge_r]
                    shift = 1
                else:
                    ext = [recv_l[k, 4 * NQ + at] * edge_l] + own
                    ext = ext + [recv_r[k, 2 * at] * edge_r, recv_r[k, 2 * at + 1] * edge_r]
                    shift = 0
                diff = [ext[j + 1] - ext[j] for j in range(RB + 2)]
                second = [diff[j + 1] - diff[j] for j in range(RB + 1)]
                faces = []
                for j in range(RB + 1):
                    nu = cosine * gx[j, freqs, :]
                    faces.append(face_of(nu, ext[j + shift], diff[j + shift], second[j]))
                for r in range(RB):
                    value = own[r] - (faces[r + 1] - faces[r])
                    nu = sine * gy[r, freqs, :]
                    if q in (0, 1):
                        behind = value - jnp.where(first_lane, 0.0, pltpu.roll(value, 1, 1))
                        ahead = pltpu.roll(behind, NY - 1, 1)
                        face = face_of(nu, value, ahead, ahead - behind)
                    else:
                        ahead = jnp.where(last_lane, 0.0, pltpu.roll(value, NY - 1, 1)) - value
                        further = pltpu.roll(ahead, NY - 1, 1)
                        face = face_of(nu, value, ahead, further - ahead)
                    work[d + 1, r] = value - (face - pltpu.roll(face, 1, 1))
            return carry

        lax.fori_loop(0, NQ, along_x_and_y, 0)
        for r in range(RB):
            work[0, r] = work[ND, r]
            work[ND + 1, r] = work[1, r]
            work[ND + 2, r] = work[2, r]

        def turn_face(d, r, base, diff, second, second_next):
            nu = trig[3 * ND + d] * rx[r, freqs, :] - trig[2 * ND + d] * ry[r, freqs, :]
            return face_of(nu, base, diff, jnp.where(nu >= 0.0, second, second_next))

        carry = []
        for r in range(RB):
            e34, e35, e0, e1 = work[ND - 1, r], work[ND, r], work[1, r], work[2, r]
            d34, d35, d0 = e35 - e34, e0 - e35, e1 - e0
            face = turn_face(ND - 1, r, e35, d35, d35 - d34, d0 - d35)
            carry.append((e0, e1, d0, d0 - d35, face))
        carry = tuple(carry)
        for q in range(4):

            def along_directions(i, state, q=q):
                d = q * NQ + i
                made = []
                later = []
                for r in range(RB):
                    e0, e1, diff, second, face_before = state[r]
                    e2 = work[d + 3, r]
                    diff_next = e2 - e1
                    second_next = diff_next - diff
                    face = turn_face(d, r, e0, diff, second, second_next)
                    made.append((e0 - (face - face_before)) * mask_v[r])
                    later.append((e1, e2, diff_next, second_next, face))
                emit(q, i, d, made)
                return tuple(later)

            carry = lax.fori_loop(0, NQ, along_directions, carry)

    def middle(k, carry):
        b = lax.rem(k, blocks)

        def emit(q, i, d, rows):
            for r in range(RB):
                energy[b, d, r] = rows[r]
            pack(q, i, k + blocks, rows)

        passes(k, b, emit)
        to_left(k + blocks).start()
        to_right(k + blocks).start()
        return carry

    lax.fori_loop(0, (SUBSTEPS - 1) * blocks, middle, 0)

    def store(b, r):
        rows = pl.ds(pl.multiple_of(b * rows_b, rows_b), rows_b)
        return pltpu.make_async_copy(out_v.at[r, rows], out.at[rows, lanes(r)], store_sem.at[b, r])

    def final(b, carry):
        def emit(q, i, d, rows):
            for r in range(RB):
                out_v[r, pl.ds(b * rows_b + d, FB, stride=ND), :] = rows[r]

        passes(b + (SUBSTEPS - 1) * blocks, b, emit)
        for r in range(RB):
            store(b, r).start()
        return carry

    lax.fori_loop(0, blocks, final, 0)

    def drain(k, carry):
        to_left(k).wait_send()
        to_right(k).wait_send()
        return carry

    lax.fori_loop(0, SUBSTEPS * blocks, drain, 0)
    for b in range(blocks):
        for r in range(RB):
            store(b, r).wait()


def per_device(
    ncomp,
    nspace,
    spectrum,
    wind_field,
    coupling,
    growth,
    dissipation,
    group_speed,
    refraction,
    depths,
    sea_mask,
    depth_index,
):
    nfreq = growth.shape[0]
    blocks = nfreq // FB
    messages = SUBSTEPS * blocks
    components, points = spectrum.shape
    f32 = jnp.float32
    smem = pl.BlockSpec(memory_space=pltpu.SMEM)
    vmem = pl.BlockSpec(memory_space=pltpu.VMEM)
    hbm = pl.BlockSpec(memory_space=pl.ANY)
    dma = pltpu.SemaphoreType.DMA
    return pl.pallas_call(
        functools.partial(kernel, nfreq, ncomp, nspace),
        out_shape=jax.ShapeDtypeStruct((components, points), f32),
        in_specs=[smem] * 4 + [vmem] * 5 + [hbm] * 2,
        out_specs=hbm,
        scratch_shapes=[
            pltpu.VMEM((RB, components, NY), f32),
            pltpu.VMEM((components, components), jnp.bfloat16),
            pltpu.VMEM((components, points), jnp.bfloat16),
            pltpu.VMEM((RB, FB * ND, NY), f32),
            pltpu.VMEM((blocks, ND, RB, FB, NY), f32),
            pltpu.VMEM((ND + 3, RB, FB, NY), f32),
            pltpu.VMEM((RB, components, NY), f32),
            pltpu.VMEM((messages, SLOTS, FB, NY), f32),
            pltpu.VMEM((messages, SLOTS, FB, NY), f32),
            pltpu.VMEM((messages, SLOTS, FB, NY), f32),
            pltpu.VMEM((messages, SLOTS, FB, NY), f32),
            pltpu.VMEM((2, 2, 8, NY), jnp.int32),
            pltpu.VMEM((2, 2, 8, NY), jnp.int32),
            pltpu.VMEM((RB + 1, nfreq, NY), f32),
            pltpu.VMEM((RB, nfreq, NY), f32),
            pltpu.VMEM((RB, nfreq, NY), f32),
            pltpu.VMEM((RB, nfreq, NY), f32),
            pltpu.VMEM((RB, 8, NY), f32),
            pltpu.VMEM((2, 8, points), f32),
            pltpu.VMEM((8, points), f32),
            dma((RB,)),
            dma((blocks,)),
            dma((blocks, RB)),
            dma((messages,)),
            dma((messages,)),
            dma((messages,)),
            dma((messages,)),
            dma((2,)),
            dma((2,)),
        ],
        compiler_params=pltpu.CompilerParams(
            collective_id=0, has_side_effects=True, vmem_limit_bytes=48 * 1024 * 1024
        ),
    )(
        jnp.asarray(direction_tables()),
        growth,
        dissipation,
        depths,
        wind_field,
        group_speed,
        refraction,
        sea_mask,
        depth_index,
        spectrum,
        coupling,
    )


def solution(mesh):
    in_specs = (
        P(None, ("comp", "space")),
        P(None, ("comp", "space")),
        P(),
        P(),
        P(),
        P(),
        P(),
        P(),
        P("space", None),
        P("space", None),
    )
    out_specs = P(None, ("comp", "space"))
    body = functools.partial(per_device, mesh.shape["comp"], mesh.shape["space"])
    return jax.shard_map(body, mesh=mesh, in_specs=in_specs, out_specs=out_specs, check_vma=False)
```

time: 257 us -> 85.1 us (0.33)
  Pallas kernels: 0 us -> 75.1 us
  blocking collectives: 65.6 us -> 0 us
  waiting for transfers between devices: 64.9 us -> 0 us
  starting transfers between devices: 47.3 us -> 0 us
  other arithmetic: 37.2 us -> 0 us
  local copies, waits for them, and re-layouts: 32.7 us -> 9.51 us
  matrix products: 7.77 us -> 0 us
    pallas_call x0 -> x1, Pallas kernels: none -> 75.1 us  [per_device(): pl.pallas_call(functools.partial(kernel, nfreq, ncomp, nspace), out_shape...]
    all_to_all x1 -> x0, blocking collectives: 65.6 us -> none  [per_device(): lax.all_to_all(flattened, 'comp', split_axis=1, concat_axis=0, tiled=True)]
    ppermute x8 -> x0, waiting for transfers between devices: 58.1 us -> none  [the longest x4 35.9 us: extended(): before = lax.ppermute(last, axis, up)]
    ppermute x8 -> x0, starting transfers between devices: 38.4 us -> none  [the longest x4 27.7 us: extended(): before = lax.ppermute(last, axis, up)]
    mul x20 -> x0, other arithmetic: 32 us -> none  [the longest x9 25.1 us: face_flux(): return courant * (central - (1.0 - courant * courant) / 6.0 * curvature)]
    all_to_all x5 -> x0, local copies, waits for them, and re-layouts: 13.3 us -> none  [the longest x3 7.22 us: per_device(): lax.all_to_all(flattened, 'comp', split_axis=1, concat_axis=0, tiled=True)]
    all_to_all x1 -> x0, starting transfers between devices: 8.89 us -> none  [per_device(): lax.all_to_all(source_terms(spectrum, wind_field, coupling, growth, dissi...]
    dot_general x2 -> x0, matrix products: 7.77 us -> none  [the longest x1 7.01 us: source_terms(): jnp.dot(coupling, energy.astype(jnp.bfloat16), preferred_element_type=jnp...]
  transfers between devices with their start and end apart: 9 -> 0, of which waited for: 6 -> 0; matrix products, arithmetic and copies ran while one was open for 3% -> 0% of each run, Pallas kernels for 0% -> 0%
where the time goes in v1:
time: 85.1 us; the launch traced here: 84.7 us
  Pallas kernels  75.1 us (88%)
  local copies, waits for them, and re-layouts  9.51 us (11%)
    pallas_call x1, Pallas kernels, per_device(): pl.pallas_call(functools.partial(kernel, nfreq, ncomp, nspace), out_shape...  75.1 us
    unnamed x21, local copies, waits for them, and re-layouts  9.51 us

profile of v1, /device:TPU:24, one launch (start us, length us, event | category | flops | bytes accessed | tf_op | source)
XLA Modules:
  0.0 84.7 jit_solution(11236507656686496391)
XLA Ops:
  0.0 0.0 copy-start
  0.0 1.7 %copy-done = f32[1152,512]{1,0:T(8,128)S(1)} copy-done((f32[1152,512]{1,0:T(8,128)S(1)}, f32[1152,512]{1,0:T(8,128)}, u32[]{:S(2)}) %copy-start) | copy-done | bytes 2359320
  1.7 0.0 copy-start.1
  1.7 0.8 copy-done.1
  2.5 0.0 copy-start.2
  2.5 0.8 copy-done.2
  3.3 0.0 copy-start.3
  3.3 0.7 copy-done.3
  4.1 0.0 copy-start.4
  4.1 0.7 copy-done.4
  4.8 0.0 copy-start.5
  4.8 0.7 copy-done.5
  5.5 0.0 copy-start.6
  5.5 0.7 copy-done.6
  6.1 0.0 copy-start.7
  6.2 0.7 copy-done.7
  6.8 0.0 copy-start.8
  6.8 0.7 copy-done.8
  7.5 0.0 copy-start.9
  7.5 0.7 copy-done.9
  8.1 75.1 %shard_map.109 = f32[1152,512]{1,0:T(8,128)S(1)} custom-call(f32[144]{0:T(256)S(1)} %copy-done.6, f32[32]{0:T(128)S(1)} %copy-done.7, f32[32]{0:T(128)S(1)} %copy-done.8, f32[32]{0:T(128)S(1)} %copy-done.9, f32[2,512]{1,0:T(2,128)S(1)} %copy-done.5, f32[32,32]{1,0:T(8,128)S(1)} %copy-done.3, f32[32,32]{1,0:T(8,128)S(1)} %copy-done.4, ...), custom_call_target="tpu_custom_call" | custom-call | tf_op jit(solution)/shard_map/pallas_call | solution.py:412
  83.3 1.4 %copy.13 = f32[1152,512]{1,0:T(8,128)} copy(f32[1152,512]{1,0:T(8,128)S(1)} %shard_map.109) | data formatting | bytes 4718592
Async XLA Ops:
  0.0 1.7 %copy-start = (f32[1152,512]{1,0:T(8,128)S(1)}, f32[1152,512]{1,0:T(8,128)}, u32[]{:S(2)}) copy-start(f32[1152,512]{1,0:T(8,128)} %spectrum.1) | copy-start | bytes 7077892
  1.7 0.8 copy-start.1
  2.5 0.8 copy-start.2
  3.3 0.7 copy-start.3
  4.1 0.7 copy-start.4
  4.8 0.7 copy-start.5
  5.5 0.7 copy-start.6
  6.1 0.7 copy-start.7
  6.8 0.7 copy-start.8
  7.5 0.7 copy-start.9

commit v2 on v1

--- a/solution.py
+++ b/solution.py
@@ -35,6 +35,17 @@
     nfreq,
     ncomp,
     nspace,
+    spectrum,
+    wind_hbm,
+    coupling,
+    growth_hbm,
+    dissipation_hbm,
+    group_speed_hbm,
+    refraction_hbm,
+    depths_hbm,
+    sea_mask_hbm,
+    depth_index_hbm,
+    out,
     trig,
     growth,
     dissipation,
@@ -44,9 +55,6 @@
     refraction,
     sea_mask,
     depth_index,
-    spectrum,
-    coupling,
-    out,
     spec_v,
     coup_v,
     spec_b,
@@ -67,6 +75,7 @@
     mask_v,
     wind_v,
     ratio_v,
+    small_sem,
     load_sem,
     coup_sem,
     store_sem,
@@ -103,6 +112,24 @@
 
     for r in range(RB):
         spec_load(r).start()
+    own_tile = pl.ds(pl.multiple_of(lax.div(c * RB, 8) * 8, 8), 8)
+    small_loads = [
+        pltpu.make_async_copy(src, dst, small_sem.at[j])
+        for j, (src, dst) in enumerate(
+            (
+                (sea_mask_hbm.at[own_tile], sea_mask),
+                (depth_index_hbm.at[own_tile], depth_index),
+                (wind_hbm, wind),
+                (growth_hbm, growth),
+                (dissipation_hbm, dissipation),
+                (group_speed_hbm, group_speed),
+                (refraction_hbm, refraction),
+                (depths_hbm, depths),
+            )
+        )
+    ]
+    for load in small_loads:
+        load.start()
 
     def coup_load(b):
         rows = pl.ds(pl.multiple_of(b * rows_b, rows_b), rows_b)
@@ -111,8 +138,105 @@
     for b in range(blocks):
         coup_load(b).start()
 
-    own_mask = [sea_mask[pl.ds(c * RB + r, 1), :] for r in range(RB)]
-    own_index = [depth_index[pl.ds(c * RB + r, 1), :] for r in range(RB)]
+    for at, value in enumerate(direction_tables()):
+        trig[at] = jnp.float32(value)
+    for load in small_loads:
+        load.wait()
+
+    def to_left(k):
+        return pltpu.make_async_remote_copy(
+            src_ref=send_l.at[k],
+            dst_ref=recv_r.at[k],
+            send_sem=send_l_sem.at[k],
+            recv_sem=recv_r_sem.at[k],
+            device_id=left,
+            device_id_type=MESH,
+        )
+
+    def to_right(k):
+        return pltpu.make_async_remote_copy(
+            src_ref=send_r.at[k],
+            dst_ref=recv_l.at[k],
+            send_sem=send_r_sem.at[k],
+            recv_sem=recv_l_sem.at[k],
+            device_id=right,
+            device_id_type=MESH,
+        )
+
+    for r in range(RB):
+        spec_load(r).wait()
+
+        def cast_rows(i, acc, r=r):
+            rows = pl.ds(pl.multiple_of(i * 64, 64), 64)
+            block = spec_v[r, rows, :]
+            spec_b[rows, lanes(r)] = block.astype(jnp.bfloat16)
+            return acc + jnp.sum(block.reshape(8, 8, NY), axis=0)
+
+        acc = lax.fori_loop(0, components // 64, cast_rows, jnp.zeros((8, NY), jnp.float32))
+        average = jnp.sum(acc, axis=0, keepdims=True) * (1.0 / components)
+        ratio_v[:, lanes(r)] = jnp.broadcast_to(average / (average + 1.0), (8, NY))
+    wind_v[0] = jnp.broadcast_to(wind[0:1, :], (8, RB * NY))
+    wind_v[1] = jnp.broadcast_to(wind[1:2, :], (8, RB * NY))
+
+    def pack(q, i, k, rows):
+        if q in (0, 3):
+            at = i + (0 if q == 0 else NQ)
+            send_r[k, 2 * at] = rows[RB - 2]
+            send_r[k, 2 * at + 1] = rows[RB - 1]
+            send_l[k, 4 * NQ + at] = rows[0]
+        else:
+            at = i + (0 if q == 1 else NQ)
+            send_l[k, 2 * at] = rows[0]
+            send_l[k, 2 * at + 1] = rows[1]
+            send_r[k, 4 * NQ + at] = rows[RB - 1]
+
+    sub8 = lax.broadcasted_iota(jnp.int32, (FB, NY), 0)
+
+    def by_freq(table, b):
+        values = jnp.zeros((FB, NY), jnp.float32)
+        for j in range(FB):
+            values = jnp.where(sub8 == j, table[b * FB + j], values)
+        return values
+
+    def source(b):
+        coup_load(b).wait()
+        rows = pl.ds(pl.multiple_of(b * rows_b, rows_b), rows_b)
+        product = jnp.dot(coup_v[rows, :], spec_b[...], preferred_element_type=jnp.float32)
+        for r in range(RB):
+            nonlin[r] = product[:, lanes(r)]
+        grow = by_freq(growth, b)
+        damp = by_freq(dissipation, b)
+        damps = [damp * ratio_v[:, lanes(r)] for r in range(RB)]
+
+        def directions(i, inner):
+            for q in range(4):
+                d = q * NQ + i
+                cosine = trig[d]
+                sine = trig[ND + d]
+                made = []
+                for r in range(RB):
+                    forcing = jnp.maximum(cosine * wind_v[0, :, lanes(r)] + sine * wind_v[1, :, lanes(r)], 0.0)
+                    value = spec_v[r, pl.ds(b * rows_b + d, FB, stride=ND), :]
+                    extra = nonlin[r, pl.ds(d, FB, stride=ND), :]
+                    value = value + (grow * (forcing * forcing) - damps[r]) * value + 0.25 * extra
+                    energy[b, d, r] = value
+                    made.append(value)
+                pack(q, i, b, made)
+            return inner
+
+        lax.fori_loop(0, NQ, directions, 0, unroll=3)
+
+    def source_and_send(b, carry):
+        source(b)
+        to_left(b).start()
+        to_right(b).start()
+        return carry
+
+    source(0)
+
+    row0 = lax.rem(c * RB, 8)
+    own_mask = [sea_mask[pl.ds(row0 + r, 1), :] for r in range(RB)]
+    own_index = [depth_index[pl.ds(row0 + r, 1), :] for r in range(RB)]
     for side, r in ((0, 0), (1, RB - 1)):
         coast_out[side, 0] = jnp.broadcast_to(own_mask[r], (8, NY))
         coast_out[side, 1] = jnp.broadcast_to(own_index[r], (8, NY))
@@ -132,40 +256,9 @@
     for side in range(2):
         coast_copy(side).start()
 
-    def to_left(k):
-        return pltpu.make_async_remote_copy(
-            src_ref=send_l.at[k],
-            dst_ref=recv_r.at[k],
-            send_sem=send_l_sem.at[k],
-            recv_sem=recv_r_sem.at[k],
-            device_id=left,
-            device_id_type=MESH,
-        )
-
-    def to_right(k):
-        return pltpu.make_async_remote_copy(
-            src_ref=send_r.at[k],
-            dst_ref=recv_l.at[k],
-            send_sem=send_r_sem.at[k],
-            recv_sem=recv_l_sem.at[k],
-            device_id=right,
-            device_id_type=MESH,
-        )
-
-    for r in range(RB):
-        spec_load(r).wait()
-
-        def cast_rows(i, acc, r=r):
-            rows = pl.ds(pl.multiple_of(i * 64, 64), 64)
-            block = spec_v[r, rows, :]
-            spec_b[rows, lanes(r)] = block.astype(jnp.bfloat16)
-            return acc + jnp.sum(block.reshape(8, 8, NY), axis=0)
-
-        acc = lax.fori_loop(0, components // 64, cast_rows, jnp.zeros((8, NY), jnp.float32))
-        average = jnp.sum(acc, axis=0, keepdims=True) * (1.0 / components)
-        ratio_v[:, lanes(r)] = jnp.broadcast_to(average / (average + 1.0), (8, NY))
-    wind_v[0] = jnp.broadcast_to(wind[0:1, :], (8, RB * NY))
-    wind_v[1] = jnp.broadcast_to(wind[1:2, :], (8, RB * NY))
+    to_left(0).start()
+    to_right(0).start()
+    lax.fori_loop(1, blocks, source_and_send, 0)
 
     for side in range(2):
         coast_copy(side).wait()
@@ -211,62 +304,10 @@
         ry[r] = turning[:, lanes(r)] * (0.5 * (up - down))
         mask_v[r] = jnp.broadcast_to(mask, (8, NY))
 
-    def pack(q, i, k, rows):
-        if q in (0, 3):
-            at = i + (0 if q == 0 else NQ)
-            send_r[k, 2 * at] = rows[RB - 2]
-            send_r[k, 2 * at + 1] = rows[RB - 1]
-            send_l[k, 4 * NQ + at] = rows[0]
-        else:
-            at = i + (0 if q == 1 else NQ)
-            send_l[k, 2 * at] = rows[0]
-            send_l[k, 2 * at + 1] = rows[1]
-            send_r[k, 4 * NQ + at] = rows[RB - 1]
-
-    sub8 = lax.broadcasted_iota(jnp.int32, (FB, NY), 0)
-
-    def by_freq(table, b):
-        values = jnp.zeros((FB, NY), jnp.float32)
-        for j in range(FB):
-            values = jnp.where(sub8 == j, table[b * FB + j], values)
-        return values
-
-    def source(b, carry):
-        coup_load(b).wait()
-        rows = pl.ds(pl.multiple_of(b * rows_b, rows_b), rows_b)
-        product = jnp.dot(coup_v[rows, :], spec_b[...], preferred_element_type=jnp.float32)
-        for r in range(RB):
-            nonlin[r] = product[:, lanes(r)]
-        grow = by_freq(growth, b)
-        damp = by_freq(dissipation, b)
-        damps = [damp * ratio_v[:, lanes(r)] for r in range(RB)]
-
-        def directions(i, inner):
-            for q in range(4):
-                d = q * NQ + i
-                cosine = trig[d]
-                sine = trig[ND + d]
-                made = []
-                for r in range(RB):
-                    forcing = jnp.maximum(cosine * wind_v[0, :, lanes(r)] + sine * wind_v[1, :, lanes(r)], 0.0)
-                    value = spec_v[r, pl.ds(b * rows_b + d, FB, stride=ND), :]
-                    extra = nonlin[r, pl.ds(d, FB, stride=ND), :]
-                    value = value + (grow * (forcing * forcing) - damps[r]) * value + 0.25 * extra
-                    energy[b, d, r] = value
-                    made.append(value)
-                pack(q, i, b, made)
-            return inner
-
-        lax.fori_loop(0, NQ, directions, 0)
-        to_left(b).start()
-        to_right(b).start()
-        return carry
-
-    lax.fori_loop(0, blocks, source, 0)
 
     lane8 = lax.broadcasted_iota(jnp.int32, (FB, NY), 1)
     first_lane = lane8 == 0
-    last_lane = lane8 == NY - 1
+    last_lanes = lane8 >= NY - 2
 
     def passes(k, b, emit):
         to_left(k).wait_recv()
@@ -299,16 +340,17 @@
                     nu = sine * gy[r, freqs, :]
                     if q in (0, 1):
                         behind = value - jnp.where(first_lane, 0.0, pltpu.roll(value, 1, 1))
-                        ahead = pltpu.roll(behind, NY - 1, 1)
+                        ahead = pltpu.roll(value, NY - 1, 1) - value
                         face = face_of(nu, value, ahead, ahead - behind)
                     else:
-                        ahead = jnp.where(last_lane, 0.0, pltpu.roll(value, NY - 1, 1)) - value
-                        further = pltpu.roll(ahead, NY - 1, 1)
-                        face = face_of(nu, value, ahead, further - ahead)
+                        next1 = pltpu.roll(value, NY - 1, 1)
+                        next2 = jnp.where(last_lanes, 0.0, pltpu.roll(value, NY - 2, 1))
+                        ahead = next1 - value
+                        face = face_of(nu, value, ahead, next2 - next1 - ahead)
                     work[d + 1, r] = value - (face - pltpu.roll(face, 1, 1))
             return carry
 
-        lax.fori_loop(0, NQ, along_x_and_y, 0)
+        lax.fori_loop(0, NQ, along_x_and_y, 0, unroll=3)
         for r in range(RB):
             work[0, r] = work[ND, r]
             work[ND + 1, r] = work[1, r]
@@ -342,7 +384,7 @@
                 emit(q, i, d, made)
                 return tuple(later)
 
-            carry = lax.fori_loop(0, NQ, along_directions, carry)
+            carry = lax.fori_loop(0, NQ, along_directions, carry, unroll=3)
 
     def middle(k, carry):
         b = lax.rem(k, blocks)
@@ -384,6 +426,21 @@
     for b in range(blocks):
         for r in range(RB):
             store(b, r).wait()
+
+
+def hand_on(moved, out, load_sems, store_sems, buf):
+    chunks = load_sems.shape[0]
+    rows = moved.shape[0] // chunks
+    at = [pl.ds(j * rows, rows) for j in range(chunks)]
+    loads = [pltpu.make_async_copy(moved.at[at[j]], buf.at[at[j]], load_sems.at[j]) for j in range(chunks)]
+    stores = [pltpu.make_async_copy(buf.at[at[j]], out.at[at[j]], store_sems.at[j]) for j in range(chunks)]
+    for copy in loads:
+        copy.start()
+    for load, copy in zip(loads, stores):
+        load.wait()
+        copy.start()
+    for copy in stores:
+        copy.wait()
 
 
 def per_device(
@@ -405,16 +462,23 @@
     messages = SUBSTEPS * blocks
     components, points = spectrum.shape
     f32 = jnp.float32
-    smem = pl.BlockSpec(memory_space=pltpu.SMEM)
-    vmem = pl.BlockSpec(memory_space=pltpu.VMEM)
     hbm = pl.BlockSpec(memory_space=pl.ANY)
     dma = pltpu.SemaphoreType.DMA
-    return pl.pallas_call(
+    moved = pl.pallas_call(
         functools.partial(kernel, nfreq, ncomp, nspace),
         out_shape=jax.ShapeDtypeStruct((components, points), f32),
-        in_specs=[smem] * 4 + [vmem] * 5 + [hbm] * 2,
+        in_specs=[hbm] * 10,
         out_specs=hbm,
         scratch_shapes=[
+            pltpu.SMEM((4 * ND,), f32),
+            pltpu.SMEM(growth.shape, f32),
+            pltpu.SMEM(dissipation.shape, f32),
+            pltpu.SMEM(depths.shape, f32),
+            pltpu.VMEM(wind_field.shape, f32),
+            pltpu.VMEM(group_speed.shape, f32),
+            pltpu.VMEM(refraction.shape, f32),
+            pltpu.VMEM((8, NY), jnp.int32),
+            pltpu.VMEM((8, NY), jnp.int32),
             pltpu.VMEM((RB, components, NY), f32),
             pltpu.VMEM((components, components), jnp.bfloat16),
             pltpu.VMEM((components, points), jnp.bfloat16),
@@ -435,6 +499,7 @@
             pltpu.VMEM((RB, 8, NY), f32),
             pltpu.VMEM((2, 8, points), f32),
             pltpu.VMEM((8, points), f32),
+            dma((8,)),
             dma((RB,)),
             dma((blocks,)),
             dma((blocks, RB)),
@@ -446,21 +511,28 @@
             dma((2,)),
         ],
         compiler_params=pltpu.CompilerParams(
-            collective_id=0, has_side_effects=True, vmem_limit_bytes=48 * 1024 * 1024
+            collective_id=0, has_side_effects=True, vmem_limit_bytes=64 * 1024 * 1024 - 4096
         ),
     )(
-        jnp.asarray(direction_tables()),
+        spectrum,
+        wind_field,
+        coupling,
         growth,
         dissipation,
-        depths,
-        wind_field,
         group_speed,
         refraction,
+        depths,
         sea_mask,
         depth_index,
-        spectrum,
-        coupling,
     )
+    chunks = 8
+    return pl.pallas_call(
+        hand_on,
+        out_shape=jax.ShapeDtypeStruct((components, points), f32),
+        in_specs=[hbm],
+        out_specs=hbm,
+        scratch_shapes=[dma((chunks,)), dma((chunks,)), pltpu.VMEM((components, points), f32)],
+    )(moved)
 
 
 def solution(mesh):

time: 85.1 us -> 73 us (0.86)
  local copies, waits for them, and re-layouts: 9.51 us -> 0 us
  Pallas kernels: 75.1 us -> 72.9 us
    unnamed x21 -> x0, local copies, waits for them, and re-layouts: 9.51 us -> none
    pallas_call x1, Pallas kernels: 75.1 us -> 70.4 us  [per_device(): pl.pallas_call(functools.partial(kernel, nfreq, ncomp, nspace), out_shape...]
    pallas_call x0 -> x1, Pallas kernels: none -> 2.49 us  [per_device(): pl.pallas_call(hand_on, out_shape=jax.ShapeDtypeStruct((components, point...]
where the time goes in v2:
time: 73 us; the launch traced here: 72.9 us
  Pallas kernels  72.9 us (100%)
    pallas_call x1, Pallas kernels, per_device(): pl.pallas_call(functools.partial(kernel, nfreq, ncomp, nspace), out_shape...  70.4 us
    pallas_call x1, Pallas kernels, per_device(): pl.pallas_call(hand_on, out_shape=jax.ShapeDtypeStruct((components, point...  2.49 us

profile of v2, /device:TPU:24, one launch (start us, length us, event | category | flops | bytes accessed | tf_op | source)
XLA Modules:
  0.0 72.9 jit_solution(17893903004078475555)
XLA Ops:
  0.0 70.4 %shard_map.100.moved = f32[1152,512]{1,0:T(8,128)} custom-call(f32[1152,512]{1,0:T(8,128)} %spectrum.1, f32[2,512]{1,0:T(2,128)} %wind_hbm.1, bf16[1152,1152]{1,0:T(8,128)(2,1)} %coupling.1, f32[32]{0:T(128)} %growth_hbm.1, f32[32]{0:T(128)} %dissipation_hbm.1, f32[32,32]{1,0:T(8,128)} %group_speed_hbm.1, f32[32,32]{1,0:T(8,128)} %refraction_hbm.1, ...), custom_call_target="tpu_custom_call" | custom-call | tf_op jit(solution)/shard_map/pallas_call | solution.py:467
  70.4 2.5 %shard_map.101 = f32[1152,512]{1,0:T(8,128)} custom-call(f32[1152,512]{1,0:T(8,128)} %shard_map.100.moved), custom_call_target="tpu_custom_call" | custom-call | tf_op jit(solution)/shard_map/pallas_call | solution.py:529

commit v3 on v2

--- a/solution.py
+++ b/solution.py
@@ -15,6 +15,7 @@
 SUBSTEPS = 3
 FB = 8
 SLOTS = 6 * NQ
+PAIRS = ((2, 3), (0, 1))
 MESH = pl.DeviceIdType.MESH
 
 
@@ -110,8 +111,6 @@
     def spec_load(r):
         return pltpu.make_async_copy(spectrum.at[:, lanes(r)], spec_v.at[r], load_sem.at[r])
 
-    for r in range(RB):
-        spec_load(r).start()
     own_tile = pl.ds(pl.multiple_of(lax.div(c * RB, 8) * 8, 8), 8)
     small_loads = [
         pltpu.make_async_copy(src, dst, small_sem.at[j])
@@ -135,8 +134,9 @@
         rows = pl.ds(pl.multiple_of(b * rows_b, rows_b), rows_b)
         return pltpu.make_async_copy(coupling.at[rows], coup_v.at[rows], coup_sem.at[b])
 
-    for b in range(blocks):
-        coup_load(b).start()
+    coup_load(0).start()
+    for r in PAIRS[0]:
+        spec_load(r).start()
 
     for at, value in enumerate(direction_tables()):
         trig[at] = jnp.float32(value)
@@ -163,32 +163,24 @@
             device_id_type=MESH,
         )
 
-    for r in range(RB):
-        spec_load(r).wait()
-
-        def cast_rows(i, acc, r=r):
-            rows = pl.ds(pl.multiple_of(i * 64, 64), 64)
-            block = spec_v[r, rows, :]
-            spec_b[rows, lanes(r)] = block.astype(jnp.bfloat16)
-            return acc + jnp.sum(block.reshape(8, 8, NY), axis=0)
-
-        acc = lax.fori_loop(0, components // 64, cast_rows, jnp.zeros((8, NY), jnp.float32))
-        average = jnp.sum(acc, axis=0, keepdims=True) * (1.0 / components)
-        ratio_v[:, lanes(r)] = jnp.broadcast_to(average / (average + 1.0), (8, NY))
     wind_v[0] = jnp.broadcast_to(wind[0:1, :], (8, RB * NY))
     wind_v[1] = jnp.broadcast_to(wind[1:2, :], (8, RB * NY))
 
-    def pack(q, i, k, rows):
+    def pack_right(q, i, k, rows):
+        at = i + (0 if q in (0, 1) else NQ)
         if q in (0, 3):
-            at = i + (0 if q == 0 else NQ)
             send_r[k, 2 * at] = rows[RB - 2]
             send_r[k, 2 * at + 1] = rows[RB - 1]
+        else:
+            send_r[k, 4 * NQ + at] = rows[RB - 1]
+
+    def pack_left(q, i, k, rows):
+        at = i + (0 if q in (0, 1) else NQ)
+        if q in (0, 3):
             send_l[k, 4 * NQ + at] = rows[0]
         else:
-            at = i + (0 if q == 1 else NQ)
             send_l[k, 2 * at] = rows[0]
             send_l[k, 2 * at + 1] = rows[1]
-            send_r[k, 4 * NQ + at] = rows[RB - 1]
 
     sub8 = lax.broadcasted_iota(jnp.int32, (FB, NY), 0)
 
@@ -198,41 +190,64 @@
             values = jnp.where(sub8 == j, table[b * FB + j], values)
         return values
 
-    def source(b):
-        coup_load(b).wait()
+    def prepare(r):
+        spec_load(r).wait()
+
+        def cast_rows(i, acc):
+            rows = pl.ds(pl.multiple_of(i * 64, 64), 64)
+            block = spec_v[r, rows, :]
+            spec_b[rows, lanes(r)] = block.astype(jnp.bfloat16)
+            return acc + jnp.sum(block.reshape(8, 8, NY), axis=0)
+
+        acc = lax.fori_loop(0, components // 64, cast_rows, jnp.zeros((8, NY), jnp.float32))
+        average = jnp.sum(acc, axis=0, keepdims=True) * (1.0 / components)
+        ratio_v[:, lanes(r)] = jnp.broadcast_to(average / (average + 1.0), (8, NY))
+
+    def source(b, pair):
         rows = pl.ds(pl.multiple_of(b * rows_b, rows_b), rows_b)
-        product = jnp.dot(coup_v[rows, :], spec_b[...], preferred_element_type=jnp.float32)
-        for r in range(RB):
-            nonlin[r] = product[:, lanes(r)]
+        columns = slice(pair[0] * NY, (pair[-1] + 1) * NY)
+        product = jnp.dot(coup_v[rows, :], spec_b[:, columns], preferred_element_type=jnp.float32)
+        for at, r in enumerate(pair):
+            nonlin[r] = product[:, lanes(at)]
         grow = by_freq(growth, b)
         damp = by_freq(dissipation, b)
-        damps = [damp * ratio_v[:, lanes(r)] for r in range(RB)]
+        damps = {r: damp * ratio_v[:, lanes(r)] for r in pair}
 
         def directions(i, inner):
             for q in range(4):
                 d = q * NQ + i
                 cosine = trig[d]
                 sine = trig[ND + d]
-                made = []
-                for r in range(RB):
+                made = {}
+                for r in pair:
                     forcing = jnp.maximum(cosine * wind_v[0, :, lanes(r)] + sine * wind_v[1, :, lanes(r)], 0.0)
                     value = spec_v[r, pl.ds(b * rows_b + d, FB, stride=ND), :]
                     extra = nonlin[r, pl.ds(d, FB, stride=ND), :]
                     value = value + (grow * (forcing * forcing) - damps[r]) * value + 0.25 * extra
                     energy[b, d, r] = value
-                    made.append(value)
-                pack(q, i, b, made)
+                    made[r] = value
+                if pair == PAIRS[0]:
+                    pack_right(q, i, b, made)
+                else:
+                    pack_left(q, i, b, made)
             return inner
 
         lax.fori_loop(0, NQ, directions, 0, unroll=3)
 
     def source_and_send(b, carry):
-        source(b)
+        coup_load(b).wait()
+        source(b, PAIRS[0])
+        to_right(b).start()
+        source(b, PAIRS[1])
         to_left(b).start()
-        to_right(b).start()
         return carry
 
-    source(0)
+    prepare(PAIRS[0][0])
+    for r in PAIRS[1]:
+        spec_load(r).start()
+    prepare(PAIRS[0][1])
+    coup_load(0).wait()
+    source(0, PAIRS[0])
 
     row0 = lax.rem(c * RB, 8)
     own_mask = [sea_mask[pl.ds(row0 + r, 1), :] for r in range(RB)]
@@ -256,8 +271,13 @@
     for side in range(2):
         coast_copy(side).start()
 
+    to_right(0).start()
+    for r in PAIRS[1]:
+        prepare(r)
+    for b in range(1, blocks):
+        coup_load(b).start()
+    source(0, PAIRS[1])
     to_left(0).start()
-    to_right(0).start()
     lax.fori_loop(1, blocks, source_and_send, 0)
 
     for side in range(2):
@@ -392,11 +412,12 @@
         def emit(q, i, d, rows):
             for r in range(RB):
                 energy[b, d, r] = rows[r]
-            pack(q, i, k + blocks, rows)
+            pack_right(q, i, k + blocks, rows)
+            pack_left(q, i, k + blocks, rows)
 
         passes(k, b, emit)
+        to_right(k + blocks).start()
         to_left(k + blocks).start()
-        to_right(k + blocks).start()
         return carry
 
     lax.fori_loop(0, (SUBSTEPS - 1) * blocks, middle, 0)

time: 73 us -> 70.8 us (0.970)
  Pallas kernels: 72.9 us -> 70.6 us
    pallas_call x1, Pallas kernels: 70.4 us -> 68.1 us  [per_device(): pl.pallas_call(functools.partial(kernel, nfreq, ncomp, nspace), out_shape...]
where the time goes in v3:
time: 70.8 us; the launch traced here: 70.6 us
  Pallas kernels  70.6 us (100%)
    pallas_call x1, Pallas kernels, per_device(): pl.pallas_call(functools.partial(kernel, nfreq, ncomp, nspace), out_shape...  68.1 us
    pallas_call x1, Pallas kernels, per_device(): pl.pallas_call(hand_on, out_shape=jax.ShapeDtypeStruct((components, point...  2.49 us

profile of v3, /device:TPU:24, one launch (start us, length us, event | category | flops | bytes accessed | tf_op | source)
XLA Modules:
  0.0 70.6 jit_solution(9722279702082039853)
XLA Ops:
  0.0 68.1 %shard_map.100.moved = f32[1152,512]{1,0:T(8,128)} custom-call(f32[1152,512]{1,0:T(8,128)} %spectrum.1, f32[2,512]{1,0:T(2,128)} %wind_hbm.1, bf16[1152,1152]{1,0:T(8,128)(2,1)} %coupling.1, f32[32]{0:T(128)} %growth_hbm.1, f32[32]{0:T(128)} %dissipation_hbm.1, f32[32,32]{1,0:T(8,128)} %group_speed_hbm.1, f32[32,32]{1,0:T(8,128)} %refraction_hbm.1, ...), custom_call_target="tpu_custom_call" | custom-call | tf_op jit(solution)/shard_map/pallas_call | solution.py:488
  68.1 2.5 %shard_map.101 = f32[1152,512]{1,0:T(8,128)} custom-call(f32[1152,512]{1,0:T(8,128)} %shard_map.100.moved), custom_call_target="tpu_custom_call" | custom-call | tf_op jit(solution)/shard_map/pallas_call | solution.py:550

commit v4 on v3

--- a/solution.py
+++ b/solution.py
@@ -15,6 +15,7 @@
 SUBSTEPS = 3
 FB = 8
 SLOTS = 6 * NQ
+LEFT_LAG = 1
 PAIRS = ((2, 3), (0, 1))
 MESH = pl.DeviceIdType.MESH
 
@@ -62,7 +63,6 @@
     nonlin,
     energy,
     work,
-    out_v,
     send_l,
     send_r,
     recv_l,
@@ -79,7 +79,6 @@
     small_sem,
     load_sem,
     coup_sem,
-    store_sem,
     send_l_sem,
     send_r_sem,
     recv_l_sem,
@@ -234,13 +233,19 @@
 
         lax.fori_loop(0, NQ, directions, 0, unroll=3)
 
-    def source_and_send(b, carry):
+    def source_right(b, carry):
         coup_load(b).wait()
         source(b, PAIRS[0])
         to_right(b).start()
+        return carry
+
+    def source_left(b, carry):
         source(b, PAIRS[1])
         to_left(b).start()
         return carry
+
+    def source_both(b, carry):
+        return source_left(b - LEFT_LAG, source_right(b, carry))
 
     prepare(PAIRS[0][0])
     for r in PAIRS[1]:
@@ -272,13 +277,13 @@
         coast_copy(side).start()
 
     to_right(0).start()
+    for b in range(1, blocks):
+        coup_load(b).start()
+    lax.fori_loop(1, LEFT_LAG, source_right, 0)
     for r in PAIRS[1]:
         prepare(r)
-    for b in range(1, blocks):
-        coup_load(b).start()
-    source(0, PAIRS[1])
-    to_left(0).start()
-    lax.fori_loop(1, blocks, source_and_send, 0)
+    lax.fori_loop(LEFT_LAG, blocks, source_both, 0)
+    lax.fori_loop(blocks - LEFT_LAG, blocks, source_left, 0)
 
     for side in range(2):
         coast_copy(side).wait()
@@ -422,18 +427,12 @@
 
     lax.fori_loop(0, (SUBSTEPS - 1) * blocks, middle, 0)
 
-    def store(b, r):
-        rows = pl.ds(pl.multiple_of(b * rows_b, rows_b), rows_b)
-        return pltpu.make_async_copy(out_v.at[r, rows], out.at[rows, lanes(r)], store_sem.at[b, r])
-
     def final(b, carry):
         def emit(q, i, d, rows):
             for r in range(RB):
-                out_v[r, pl.ds(b * rows_b + d, FB, stride=ND), :] = rows[r]
+                out[r, pl.ds(b * rows_b + d, FB, stride=ND), :] = rows[r]
 
         passes(b + (SUBSTEPS - 1) * blocks, b, emit)
-        for r in range(RB):
-            store(b, r).start()
         return carry
 
     lax.fori_loop(0, blocks, final, 0)
@@ -444,23 +443,23 @@
         return carry
 
     lax.fori_loop(0, SUBSTEPS * blocks, drain, 0)
-    for b in range(blocks):
-        for r in range(RB):
-            store(b, r).wait()
-
-
-def hand_on(moved, out, load_sems, store_sems, buf):
-    chunks = load_sems.shape[0]
-    rows = moved.shape[0] // chunks
-    at = [pl.ds(j * rows, rows) for j in range(chunks)]
-    loads = [pltpu.make_async_copy(moved.at[at[j]], buf.at[at[j]], load_sems.at[j]) for j in range(chunks)]
-    stores = [pltpu.make_async_copy(buf.at[at[j]], out.at[at[j]], store_sems.at[j]) for j in range(chunks)]
-    for copy in loads:
+
+
+def hand_on(moved, out, sems):
+    chunks = sems.shape[1]
+    rows = moved.shape[1] // chunks
+    copies = [
+        pltpu.make_async_copy(
+            moved.at[r, pl.ds(j * rows, rows)],
+            out.at[pl.ds(j * rows, rows), r * NY : (r + 1) * NY],
+            sems.at[r, j],
+        )
+        for r in range(RB)
+        for j in range(chunks)
+    ]
+    for copy in copies:
         copy.start()
-    for load, copy in zip(loads, stores):
-        load.wait()
-        copy.start()
-    for copy in stores:
+    for copy in copies:
         copy.wait()
 
 
@@ -487,9 +486,9 @@
     dma = pltpu.SemaphoreType.DMA
     moved = pl.pallas_call(
         functools.partial(kernel, nfreq, ncomp, nspace),
-        out_shape=jax.ShapeDtypeStruct((components, points), f32),
+        out_shape=pltpu.VMEM((RB, components, NY), f32),
         in_specs=[hbm] * 10,
-        out_specs=hbm,
+        out_specs=pl.BlockSpec(memory_space=pltpu.VMEM),
         scratch_shapes=[
             pltpu.SMEM((4 * ND,), f32),
             pltpu.SMEM(growth.shape, f32),
@@ -506,7 +505,6 @@
             pltpu.VMEM((RB, FB * ND, NY), f32),
             pltpu.VMEM((blocks, ND, RB, FB, NY), f32),
             pltpu.VMEM((ND + 3, RB, FB, NY), f32),
-            pltpu.VMEM((RB, components, NY), f32),
             pltpu.VMEM((messages, SLOTS, FB, NY), f32),
             pltpu.VMEM((messages, SLOTS, FB, NY), f32),
             pltpu.VMEM((messages, SLOTS, FB, NY), f32),
@@ -523,7 +521,6 @@
             dma((8,)),
             dma((RB,)),
             dma((blocks,)),
-            dma((blocks, RB)),
             dma((messages,)),
             dma((messages,)),
             dma((messages,)),
@@ -532,28 +529,32 @@
             dma((2,)),
         ],
         compiler_params=pltpu.CompilerParams(
-            collective_id=0, has_side_effects=True, vmem_limit_bytes=64 * 1024 * 1024 - 4096
+            collective_id=0, has_side_effects=True, vmem_limit_bytes=48 * 1024 * 1024
         ),
     )(
-        spectrum,
-        wind_field,
-        coupling,
-        growth,
-        dissipation,
-        group_speed,
-        refraction,
-        depths,
-        sea_mask,
-        depth_index,
+        *[
+            pltpu.with_memory_space_constraint(operand, pltpu.HBM)
+            for operand in (
+                spectrum,
+                wind_field,
+                coupling,
+                growth,
+                dissipation,
+                group_speed,
+                refraction,
+                depths,
+                sea_mask,
+                depth_index,
+            )
+        ]
     )
-    chunks = 8
     return pl.pallas_call(
         hand_on,
         out_shape=jax.ShapeDtypeStruct((components, points), f32),
-        in_specs=[hbm],
+        in_specs=[pl.BlockSpec(memory_space=pltpu.VMEM)],
         out_specs=hbm,
-        scratch_shapes=[dma((chunks,)), dma((chunks,)), pltpu.VMEM((components, points), f32)],
-    )(moved)
+        scratch_shapes=[dma((RB, 1))],
+    )(pltpu.with_memory_space_constraint(moved, pltpu.VMEM))
 
 
 def solution(mesh):

time: 70.8 us -> 69 us (0.975)
  the two profiles are of different devices: /device:TPU:24 before, /device:TPU:1 now
where the time goes in v4:
time: 69 us; the launch traced here: 68.9 us
  Pallas kernels  68.8 us (100%)
    pallas_call x1, Pallas kernels, per_device(): pl.pallas_call(functools.partial(kernel, nfreq, ncomp, nspace), out_shape...  67.4 us
    pallas_call x1, Pallas kernels, per_device(): pl.pallas_call(hand_on, out_shape=jax.ShapeDtypeStruct((components, point...  1.43 us

profile of v4, /device:TPU:1, one launch (start us, length us, event | category | flops | bytes accessed | tf_op | source)
XLA Modules:
  0.0 68.9 jit_solution(16551146227131904302)
XLA Ops:
  0.0 67.4 %shard_map.100.moved = f32[4,1152,128]{2,1,0:T(8,128)S(1)} custom-call(f32[1152,512]{1,0:T(8,128)} %spectrum.1, f32[2,512]{1,0:T(2,128)} %wind_hbm.1, bf16[1152,1152]{1,0:T(8,128)(2,1)} %coupling.1, f32[32]{0:T(128)} %growth_hbm.1, f32[32]{0:T(128)} %dissipation_hbm.1, f32[32,32]{1,0:T(8,128)} %group_speed_hbm.1, f32[32,32]{1,0:T(8,128)} %refraction_hbm.1, ...), custom_call_target="tpu_custom_call" | custom-call | tf_op jit(solution)/shard_map/pallas_call | solution.py:487
  67.4 1.4 %shard_map.101 = f32[1152,512]{1,0:T(8,128)} custom-call(f32[4,1152,128]{2,1,0:T(8,128)S(1)} %shard_map.100.moved), custom_call_target="tpu_custom_call" | custom-call | tf_op jit(solution)/shard_map/pallas_call | solution.py:551

commit v5 on v4

--- a/solution.py
+++ b/solution.py
@@ -15,8 +15,10 @@
 SUBSTEPS = 3
 FB = 8
 SLOTS = 6 * NQ
-LEFT_LAG = 1
-PAIRS = ((2, 3), (0, 1))
+LOW, HIGH = (0, 1), (2, 3)
+LINE = 8
+RIGHT_AT = (0, 2 * NQ, 3 * NQ, 4 * NQ, 6 * NQ)
+LEFT_AT = (0, NQ, 3 * NQ, 5 * NQ, 6 * NQ)
 MESH = pl.DeviceIdType.MESH
 
 
@@ -83,6 +85,10 @@
     send_r_sem,
     recv_l_sem,
     recv_r_sem,
+    part_send_l_sem,
+    part_send_r_sem,
+    part_recv_l_sem,
+    part_recv_r_sem,
     coast_send_sem,
     coast_recv_sem,
 ):
@@ -134,8 +140,6 @@
         return pltpu.make_async_copy(coupling.at[rows], coup_v.at[rows], coup_sem.at[b])
 
     coup_load(0).start()
-    for r in PAIRS[0]:
-        spec_load(r).start()
 
     for at, value in enumerate(direction_tables()):
         trig[at] = jnp.float32(value)
@@ -166,20 +170,20 @@
     wind_v[1] = jnp.broadcast_to(wind[1:2, :], (8, RB * NY))
 
     def pack_right(q, i, k, rows):
-        at = i + (0 if q in (0, 1) else NQ)
+        at = RIGHT_AT[q]
         if q in (0, 3):
-            send_r[k, 2 * at] = rows[RB - 2]
-            send_r[k, 2 * at + 1] = rows[RB - 1]
+            send_r[k, at + 2 * i] = rows[RB - 2]
+            send_r[k, at + 2 * i + 1] = rows[RB - 1]
         else:
-            send_r[k, 4 * NQ + at] = rows[RB - 1]
+            send_r[k, at + i] = rows[RB - 1]
 
     def pack_left(q, i, k, rows):
-        at = i + (0 if q in (0, 1) else NQ)
+        at = LEFT_AT[q]
         if q in (0, 3):
-            send_l[k, 4 * NQ + at] = rows[0]
+            send_l[k, at + i] = rows[0]
         else:
-            send_l[k, 2 * at] = rows[0]
-            send_l[k, 2 * at + 1] = rows[1]
+            send_l[k, at + 2 * i] = rows[0]
+            send_l[k, at + 2 * i + 1] = rows[1]
 
     sub8 = lax.broadcasted_iota(jnp.int32, (FB, NY), 0)
 
@@ -188,6 +192,30 @@
         for j in range(FB):
             values = jnp.where(sub8 == j, table[b * FB + j], values)
         return values
+
+    last = SUBSTEPS * blocks - 1
+
+    def left_part(q):
+        tiles = pl.ds(LEFT_AT[q], LEFT_AT[q + 1] - LEFT_AT[q])
+        return pltpu.make_async_remote_copy(
+            src_ref=send_l.at[last, tiles],
+            dst_ref=recv_r.at[last, tiles],
+            send_sem=part_send_l_sem.at[q],
+            recv_sem=part_recv_r_sem.at[q],
+            device_id=left,
+            device_id_type=MESH,
+        )
+
+    def right_part(q):
+        tiles = pl.ds(RIGHT_AT[q], RIGHT_AT[q + 1] - RIGHT_AT[q])
+        return pltpu.make_async_remote_copy(
+            src_ref=send_r.at[last, tiles],
+            dst_ref=recv_l.at[last, tiles],
+            send_sem=part_send_r_sem.at[q],
+            recv_sem=part_recv_l_sem.at[q],
+            device_id=right,
+            device_id_type=MESH,
+        )
 
     def prepare(r):
         spec_load(r).wait()
@@ -225,7 +253,7 @@
                     value = value + (grow * (forcing * forcing) - damps[r]) * value + 0.25 * extra
                     energy[b, d, r] = value
                     made[r] = value
-                if pair == PAIRS[0]:
+                if pair == HIGH:
                     pack_right(q, i, b, made)
                 else:
                     pack_left(q, i, b, made)
@@ -233,26 +261,41 @@
 
         lax.fori_loop(0, NQ, directions, 0, unroll=3)
 
-    def source_right(b, carry):
-        coup_load(b).wait()
-        source(b, PAIRS[0])
-        to_right(b).start()
-        return carry
-
-    def source_left(b, carry):
-        source(b, PAIRS[1])
-        to_left(b).start()
-        return carry
-
-    def source_both(b, carry):
-        return source_left(b - LEFT_LAG, source_right(b, carry))
-
-    prepare(PAIRS[0][0])
-    for r in PAIRS[1]:
-        spec_load(r).start()
-    prepare(PAIRS[0][1])
-    coup_load(0).wait()
-    source(0, PAIRS[0])
+    def open_with(first, second):
+        for r in first:
+            spec_load(r).start()
+        prepare(first[0])
+        for r in second:
+            spec_load(r).start()
+        prepare(first[1])
+        coup_load(0).wait()
+        source(0, first)
+
+    def go_on_with(first, second):
+        send_of(first, 0).start()
+        for r in second:
+            prepare(r)
+        for b in range(1, blocks):
+            coup_load(b).start()
+        source(0, second)
+        send_of(second, 0).start()
+
+        def others(b, carry):
+            coup_load(b).wait()
+            source(b, first)
+            send_of(first, b).start()
+            source(b, second)
+            send_of(second, b).start()
+            return carry
+
+        lax.fori_loop(1, blocks, others, 0)
+
+    def send_of(pair, k):
+        return to_left(k) if pair == LOW else to_right(k)
+
+    low_first = jnp.logical_and(lax.rem(c, 2) == 0, c < ncomp - LINE)
+    pl.when(low_first)(lambda: open_with(LOW, HIGH))
+    pl.when(jnp.logical_not(low_first))(lambda: open_with(HIGH, LOW))
 
     row0 = lax.rem(c * RB, 8)
     own_mask = [sea_mask[pl.ds(row0 + r, 1), :] for r in range(RB)]
@@ -276,14 +319,8 @@
     for side in range(2):
         coast_copy(side).start()
 
-    to_right(0).start()
-    for b in range(1, blocks):
-        coup_load(b).start()
-    lax.fori_loop(1, LEFT_LAG, source_right, 0)
-    for r in PAIRS[1]:
-        prepare(r)
-    lax.fori_loop(LEFT_LAG, blocks, source_both, 0)
-    lax.fori_loop(blocks - LEFT_LAG, blocks, source_left, 0)
+    pl.when(low_first)(lambda: go_on_with(LOW, HIGH))
+    pl.when(jnp.logical_not(low_first))(lambda: go_on_with(HIGH, LOW))
 
     for side in range(2):
         coast_copy(side).wait()
@@ -334,62 +371,107 @@
     first_lane = lane8 == 0
     last_lanes = lane8 >= NY - 2
 
-    def passes(k, b, emit):
-        to_left(k).wait_recv()
-        to_right(k).wait_recv()
+    def turn_face(freqs, d, r, base, diff, second, second_next):
+        nu = trig[3 * ND + d] * rx[r, freqs, :] - trig[2 * ND + d] * ry[r, freqs, :]
+        return face_of(nu, base, diff, jnp.where(nu >= 0.0, second, second_next))
+
+    def last_passes(freqs, arrive, one_quadrant, emit):
+        state = None
+        cell = 2
+        for q in range(4):
+            arrive(q)
+            one_quadrant(q)
+            if q == 3:
+                for d in range(4):
+                    for r in range(RB):
+                        work[ND + 1 + d, r] = work[1 + d, r]
+            if q == 0:
+                state = []
+                for r in range(RB):
+                    e0, e1, e2, e3 = (work[1 + d, r] for d in range(4))
+                    d0, d1, d2 = e1 - e0, e2 - e1, e3 - e2
+                    face = turn_face(freqs, 1, r, e1, d1, d1 - d0, d2 - d1)
+                    state.append((e2, e3, d2, d2 - d1, face))
+            until = (q + 1) * NQ - 2 if q < 3 else ND + 2
+            while cell < until:
+                made = []
+                for r in range(RB):
+                    e0, e1, diff, second, face_before = state[r]
+                    e2 = work[cell + 3, r]
+                    diff_next = e2 - e1
+                    second_next = diff_next - diff
+                    face = turn_face(freqs, cell % ND, r, e0, diff, second, second_next)
+                    made.append((e0 - (face - face_before)) * mask_v[r])
+                    state[r] = (e1, e2, diff_next, second_next, face)
+                emit(None, None, cell % ND, made)
+                cell += 1
+
+    def passes(k, b, emit, arrive=None):
+        if arrive is None:
+            to_left(k).wait_recv()
+            to_right(k).wait_recv()
         freqs = pl.ds(pl.multiple_of(b * FB, FB), FB)
+
+        def x_and_y(q, i):
+            d = q * NQ + i
+            cosine = trig[d]
+            sine = trig[ND + d]
+            own = [energy[b, d, r] for r in range(RB)]
+            low, high = RIGHT_AT[q], LEFT_AT[q]
+            if q in (0, 3):
+                ext = [recv_l[k, low + 2 * i] * edge_l, recv_l[k, low + 2 * i + 1] * edge_l]
+                ext = ext + own + [recv_r[k, high + i] * edge_r]
+                shift = 1
+            else:
+                ext = [recv_l[k, low + i] * edge_l] + own
+                ext = ext + [recv_r[k, high + 2 * i] * edge_r, recv_r[k, high + 2 * i + 1] * edge_r]
+                shift = 0
+            diff = [ext[j + 1] - ext[j] for j in range(RB + 2)]
+            second = [diff[j + 1] - diff[j] for j in range(RB + 1)]
+            faces = []
+            for j in range(RB + 1):
+                nu = cosine * gx[j, freqs, :]
+                faces.append(face_of(nu, ext[j + shift], diff[j + shift], second[j]))
+            for r in range(RB):
+                value = own[r] - (faces[r + 1] - faces[r])
+                nu = sine * gy[r, freqs, :]
+                if q in (0, 1):
+                    behind = value - jnp.where(first_lane, 0.0, pltpu.roll(value, 1, 1))
+                    ahead = pltpu.roll(value, NY - 1, 1) - value
+                    face = face_of(nu, value, ahead, ahead - behind)
+                else:
+                    next1 = pltpu.roll(value, NY - 1, 1)
+                    next2 = jnp.where(last_lanes, 0.0, pltpu.roll(value, NY - 2, 1))
+                    ahead = next1 - value
+                    face = face_of(nu, value, ahead, next2 - next1 - ahead)
+                work[d + 1, r] = value - (face - pltpu.roll(face, 1, 1))
 
         def along_x_and_y(i, carry):
             for q in range(4):
-                d = q * NQ + i
-                cosine = trig[d]
-                sine = trig[ND + d]
-                own = [energy[b, d, r] for r in range(RB)]
-                at = i + (0 if q in (0, 1) else NQ)
-                if q in (0, 3):
-                    ext = [recv_l[k, 2 * at] * edge_l, recv_l[k, 2 * at + 1] * edge_l]
-                    ext = ext + own + [recv_r[k, 4 * NQ + at] * edge_r]
-                    shift = 1
-                else:
-                    ext = [recv_l[k, 4 * NQ + at] * edge_l] + own
-                    ext = ext + [recv_r[k, 2 * at] * edge_r, recv_r[k, 2 * at + 1] * edge_r]
-                    shift = 0
-                diff = [ext[j + 1] - ext[j] for j in range(RB + 2)]
-                second = [diff[j + 1] - diff[j] for j in range(RB + 1)]
-                faces = []
-                for j in range(RB + 1):
-                    nu = cosine * gx[j, freqs, :]
-                    faces.append(face_of(nu, ext[j + shift], diff[j + shift], second[j]))
-                for r in range(RB):
-                    value = own[r] - (faces[r + 1] - faces[r])
-                    nu = sine * gy[r, freqs, :]
-                    if q in (0, 1):
-                        behind = value - jnp.where(first_lane, 0.0, pltpu.roll(value, 1, 1))
-                        ahead = pltpu.roll(value, NY - 1, 1) - value
-                        face = face_of(nu, value, ahead, ahead - behind)
-                    else:
-                        next1 = pltpu.roll(value, NY - 1, 1)
-                        next2 = jnp.where(last_lanes, 0.0, pltpu.roll(value, NY - 2, 1))
-                        ahead = next1 - value
-                        face = face_of(nu, value, ahead, next2 - next1 - ahead)
-                    work[d + 1, r] = value - (face - pltpu.roll(face, 1, 1))
+                x_and_y(q, i)
             return carry
 
+        def one_quadrant(q):
+            def run(i, carry):
+                x_and_y(q, i)
+                return carry
+
+            lax.fori_loop(0, NQ, run, 0, unroll=NQ)
+
+        if arrive is not None:
+            last_passes(freqs, arrive, one_quadrant, emit)
+            return
         lax.fori_loop(0, NQ, along_x_and_y, 0, unroll=3)
         for r in range(RB):
             work[0, r] = work[ND, r]
             work[ND + 1, r] = work[1, r]
             work[ND + 2, r] = work[2, r]
 
-        def turn_face(d, r, base, diff, second, second_next):
-            nu = trig[3 * ND + d] * rx[r, freqs, :] - trig[2 * ND + d] * ry[r, freqs, :]
-            return face_of(nu, base, diff, jnp.where(nu >= 0.0, second, second_next))
-
         carry = []
         for r in range(RB):
             e34, e35, e0, e1 = work[ND - 1, r], work[ND, r], work[1, r], work[2, r]
             d34, d35, d0 = e35 - e34, e0 - e35, e1 - e0
-            face = turn_face(ND - 1, r, e35, d35, d35 - d34, d0 - d35)
+            face = turn_face(freqs, ND - 1, r, e35, d35, d35 - d34, d0 - d35)
             carry.append((e0, e1, d0, d0 - d35, face))
         carry = tuple(carry)
         for q in range(4):
@@ -403,7 +485,7 @@
                     e2 = work[d + 3, r]
                     diff_next = e2 - e1
                     second_next = diff_next - diff
-                    face = turn_face(d, r, e0, diff, second, second_next)
+                    face = turn_face(freqs, d, r, e0, diff, second, second_next)
                     made.append((e0 - (face - face_before)) * mask_v[r])
                     later.append((e1, e2, diff_next, second_next, face))
                 emit(q, i, d, made)
@@ -421,28 +503,49 @@
             pack_left(q, i, k + blocks, rows)
 
         passes(k, b, emit)
-        to_right(k + blocks).start()
-        to_left(k + blocks).start()
+
+        @pl.when(k + blocks < last)
+        def _():
+            to_right(k + blocks).start()
+            to_left(k + blocks).start()
+
+        @pl.when(k + blocks == last)
+        def _():
+            for q in range(4):
+                right_part(q).start()
+                left_part(q).start()
+
         return carry
 
     lax.fori_loop(0, (SUBSTEPS - 1) * blocks, middle, 0)
 
-    def final(b, carry):
+    def emit_out(b):
         def emit(q, i, d, rows):
             for r in range(RB):
                 out[r, pl.ds(b * rows_b + d, FB, stride=ND), :] = rows[r]
 
-        passes(b + (SUBSTEPS - 1) * blocks, b, emit)
+        return emit
+
+    def final(b, carry):
+        passes(b + (SUBSTEPS - 1) * blocks, b, emit_out(b))
         return carry
 
-    lax.fori_loop(0, blocks, final, 0)
+    def arrive(q):
+        left_part(q).wait_recv()
+        right_part(q).wait_recv()
+
+    lax.fori_loop(0, blocks - 1, final, 0)
+    passes(last, blocks - 1, emit_out(blocks - 1), arrive)
 
     def drain(k, carry):
         to_left(k).wait_send()
         to_right(k).wait_send()
         return carry
 
-    lax.fori_loop(0, SUBSTEPS * blocks, drain, 0)
+    lax.fori_loop(0, last, drain, 0)
+    for q in range(4):
+        left_part(q).wait_send()
+        right_part(q).wait_send()
 
 
 def hand_on(moved, out, sems):
@@ -504,7 +607,7 @@
             pltpu.VMEM((components, points), jnp.bfloat16),
             pltpu.VMEM((RB, FB * ND, NY), f32),
             pltpu.VMEM((blocks, ND, RB, FB, NY), f32),
-            pltpu.VMEM((ND + 3, RB, FB, NY), f32),
+            pltpu.VMEM((ND + 5, RB, FB, NY), f32),
             pltpu.VMEM((messages, SLOTS, FB, NY), f32),
             pltpu.VMEM((messages, SLOTS, FB, NY), f32),
             pltpu.VMEM((messages, SLOTS, FB, NY), f32),
@@ -525,6 +628,10 @@
             dma((messages,)),
             dma((messages,)),
             dma((messages,)),
+            dma((4,)),
+            dma((4,)),
+            dma((4,)),
+            dma((4,)),
             dma((2,)),
             dma((2,)),
         ],

time: 69 us -> 68.4 us (level)
  the two profiles are of different devices: /device:TPU:1 before, /device:TPU:24 now
where the time goes in v5:
time: 68.4 us; the launch traced here: 68.3 us
  Pallas kernels  68.2 us (100%)
    pallas_call x1, Pallas kernels, per_device(): pl.pallas_call(functools.partial(kernel, nfreq, ncomp, nspace), out_shape...  66.8 us
    pallas_call x1, Pallas kernels, per_device(): pl.pallas_call(hand_on, out_shape=jax.ShapeDtypeStruct((components, point...  1.43 us

profile of v5, /device:TPU:24, one launch (start us, length us, event | category | flops | bytes accessed | tf_op | source)
XLA Modules:
  0.0 68.3 jit_solution(8785370966094588243)
XLA Ops:
  0.0 66.8 %shard_map.100.moved = f32[4,1152,128]{2,1,0:T(8,128)S(1)} custom-call(f32[1152,512]{1,0:T(8,128)} %spectrum.1, f32[2,512]{1,0:T(2,128)} %wind_hbm.1, bf16[1152,1152]{1,0:T(8,128)(2,1)} %coupling.1, f32[32]{0:T(128)} %growth_hbm.1, f32[32]{0:T(128)} %dissipation_hbm.1, f32[32,32]{1,0:T(8,128)} %group_speed_hbm.1, f32[32,32]{1,0:T(8,128)} %refraction_hbm.1, ...), custom_call_target="tpu_custom_call" | custom-call | tf_op jit(solution)/shard_map/pallas_call | solution.py:590
  66.8 1.4 %shard_map.101 = f32[1152,512]{1,0:T(8,128)} custom-call(f32[4,1152,128]{2,1,0:T(8,128)S(1)} %shard_map.100.moved), custom_call_target="tpu_custom_call" | custom-call | tf_op jit(solution)/shard_map/pallas_call | solution.py:658

commit v6 on v5

--- a/solution.py
+++ b/solution.py
@@ -10,6 +10,7 @@
 
 ND = 36
 NQ = 9
+SPARE = 40
 RB = 4
 NY = 128
 SUBSTEPS = 3
@@ -114,7 +115,9 @@
         return slice(r * NY, (r + 1) * NY)
 
     def spec_load(r):
-        return pltpu.make_async_copy(spectrum.at[:, lanes(r)], spec_v.at[r], load_sem.at[r])
+        return pltpu.make_async_copy(
+            spectrum.at[:, lanes(r)], spec_v.at[r, pl.ds(0, components)], load_sem.at[r]
+        )
 
     own_tile = pl.ds(pl.multiple_of(lax.div(c * RB, 8) * 8, 8), 8)
     small_loads = [
@@ -235,7 +238,7 @@
         columns = slice(pair[0] * NY, (pair[-1] + 1) * NY)
         product = jnp.dot(coup_v[rows, :], spec_b[:, columns], preferred_element_type=jnp.float32)
         for at, r in enumerate(pair):
-            nonlin[r] = product[:, lanes(at)]
+            nonlin[r, :rows_b] = product[:, lanes(at)]
         grow = by_freq(growth, b)
         damp = by_freq(dissipation, b)
         damps = {r: damp * ratio_v[:, lanes(r)] for r in pair}
@@ -550,7 +553,7 @@
 
 def hand_on(moved, out, sems):
     chunks = sems.shape[1]
-    rows = moved.shape[1] // chunks
+    rows = out.shape[0] // chunks
     copies = [
         pltpu.make_async_copy(
             moved.at[r, pl.ds(j * rows, rows)],
@@ -589,7 +592,7 @@
     dma = pltpu.SemaphoreType.DMA
     moved = pl.pallas_call(
         functools.partial(kernel, nfreq, ncomp, nspace),
-        out_shape=pltpu.VMEM((RB, components, NY), f32),
+        out_shape=pltpu.VMEM((RB, components + SPARE, NY), f32),
         in_specs=[hbm] * 10,
         out_specs=pl.BlockSpec(memory_space=pltpu.VMEM),
         scratch_shapes=[
@@ -602,10 +605,10 @@
             pltpu.VMEM(refraction.shape, f32),
             pltpu.VMEM((8, NY), jnp.int32),
             pltpu.VMEM((8, NY), jnp.int32),
-            pltpu.VMEM((RB, components, NY), f32),
+            pltpu.VMEM((RB, components + SPARE, NY), f32),
             pltpu.VMEM((components, components), jnp.bfloat16),
             pltpu.VMEM((components, points), jnp.bfloat16),
-            pltpu.VMEM((RB, FB * ND, NY), f32),
+            pltpu.VMEM((RB, FB * ND + SPARE, NY), f32),
             pltpu.VMEM((blocks, ND, RB, FB, NY), f32),
             pltpu.VMEM((ND + 5, RB, FB, NY), f32),
             pltpu.VMEM((messages, SLOTS, FB, NY), f32),

time: 68.4 us -> 68.4 us (level)
  no operation moved by 1% of the time
where the time goes in v6:
time: 68.4 us; the launch traced here: 68.3 us
  Pallas kernels  68.2 us (100%)
    pallas_call x1, Pallas kernels, per_device(): pl.pallas_call(functools.partial(kernel, nfreq, ncomp, nspace), out_shape...  66.8 us
    pallas_call x1, Pallas kernels, per_device(): pl.pallas_call(hand_on, out_shape=jax.ShapeDtypeStruct((components, point...  1.43 us

profile of v6, /device:TPU:24, one launch (start us, length us, event | category | flops | bytes accessed | tf_op | source)
XLA Modules:
  0.0 68.3 jit_solution(8120642692224920585)
XLA Ops:
  0.0 66.8 %shard_map.100.moved = f32[4,1192,128]{2,1,0:T(8,128)S(1)} custom-call(f32[1152,512]{1,0:T(8,128)} %spectrum.1, f32[2,512]{1,0:T(2,128)} %wind_hbm.1, bf16[1152,1152]{1,0:T(8,128)(2,1)} %coupling.1, f32[32]{0:T(128)} %growth_hbm.1, f32[32]{0:T(128)} %dissipation_hbm.1, f32[32,32]{1,0:T(8,128)} %group_speed_hbm.1, f32[32,32]{1,0:T(8,128)} %refraction_hbm.1, ...), custom_call_target="tpu_custom_call" | custom-call | tf_op jit(solution)/shard_map/pallas_call | solution.py:593
  66.8 1.4 %shard_map.101 = f32[1152,512]{1,0:T(8,128)} custom-call(f32[4,1192,128]{2,1,0:T(8,128)S(1)} %shard_map.100.moved), custom_call_target="tpu_custom_call" | custom-call | tf_op jit(solution)/shard_map/pallas_call | solution.py:661

commit v7 on v6

--- a/solution.py
+++ b/solution.py
@@ -142,7 +142,6 @@
         rows = pl.ds(pl.multiple_of(b * rows_b, rows_b), rows_b)
         return pltpu.make_async_copy(coupling.at[rows], coup_v.at[rows], coup_sem.at[b])
 
-    coup_load(0).start()
 
     for at, value in enumerate(direction_tables()):
         trig[at] = jnp.float32(value)
@@ -267,11 +266,12 @@
     def open_with(first, second):
         for r in first:
             spec_load(r).start()
+        coup_load(0).start()
         prepare(first[0])
+        prepare(first[1])
+        coup_load(0).wait()
         for r in second:
             spec_load(r).start()
-        prepare(first[1])
-        coup_load(0).wait()
         source(0, first)
 
     def go_on_with(first, second):
@@ -507,10 +507,15 @@
 
         passes(k, b, emit)
 
-        @pl.when(k + blocks < last)
+        @pl.when(jnp.logical_and(k + blocks < last, lax.rem(c, 2) == 0))
         def _():
             to_right(k + blocks).start()
             to_left(k + blocks).start()
+
+        @pl.when(jnp.logical_and(k + blocks < last, lax.rem(c, 2) == 1))
+        def _():
+            to_left(k + blocks).start()
+            to_right(k + blocks).start()
 
         @pl.when(k + blocks == last)
         def _():

time: 68.4 us -> 68.3 us (level)
  no operation moved by 1% of the time
where the time goes in v7:
time: 68.3 us; the launch traced here: 68.1 us
  Pallas kernels  68.1 us (100%)
    pallas_call x1, Pallas kernels, per_device(): pl.pallas_call(functools.partial(kernel, nfreq, ncomp, nspace), out_shape...  66.7 us
    pallas_call x1, Pallas kernels, per_device(): pl.pallas_call(hand_on, out_shape=jax.ShapeDtypeStruct((components, point...  1.43 us

profile of v7, /device:TPU:24, one launch (start us, length us, event | category | flops | bytes accessed | tf_op | source)
XLA Modules:
  0.0 68.1 jit_solution(5058005039060011068)
XLA Ops:
  0.0 66.7 %shard_map.100.moved = f32[4,1192,128]{2,1,0:T(8,128)S(1)} custom-call(f32[1152,512]{1,0:T(8,128)} %spectrum.1, f32[2,512]{1,0:T(2,128)} %wind_hbm.1, bf16[1152,1152]{1,0:T(8,128)(2,1)} %coupling.1, f32[32]{0:T(128)} %growth_hbm.1, f32[32]{0:T(128)} %dissipation_hbm.1, f32[32,32]{1,0:T(8,128)} %group_speed_hbm.1, f32[32,32]{1,0:T(8,128)} %refraction_hbm.1, ...), custom_call_target="tpu_custom_call" | custom-call | tf_op jit(solution)/shard_map/pallas_call | solution.py:598
  66.7 1.4 %shard_map.101 = f32[1152,512]{1,0:T(8,128)} custom-call(f32[4,1192,128]{2,1,0:T(8,128)S(1)} %shard_map.100.moved), custom_call_target="tpu_custom_call" | custom-call | tf_op jit(solution)/shard_map/pallas_call | solution.py:666

commit v8 on v7

--- a/solution.py
+++ b/solution.py
@@ -494,7 +494,7 @@
                 emit(q, i, d, made)
                 return tuple(later)
 
-            carry = lax.fori_loop(0, NQ, along_directions, carry, unroll=3)
+            carry = lax.fori_loop(0, NQ, along_directions, carry, unroll=NQ)
 
     def middle(k, carry):
         b = lax.rem(k, blocks)

time: 68.3 us -> 68.3 us (level)
  no operation moved by 1% of the time
where the time goes in v8:
time: 68.3 us; the launch traced here: 68.1 us
  Pallas kernels  68.1 us (100%)
    pallas_call x1, Pallas kernels, per_device(): pl.pallas_call(functools.partial(kernel, nfreq, ncomp, nspace), out_shape...  66.7 us
    pallas_call x1, Pallas kernels, per_device(): pl.pallas_call(hand_on, out_shape=jax.ShapeDtypeStruct((components, point...  1.43 us

profile of v8, /device:TPU:24, one launch (start us, length us, event | category | flops | bytes accessed | tf_op | source)
XLA Modules:
  0.0 68.1 jit_solution(17661698697176141589)
XLA Ops:
  0.0 66.7 %shard_map.100.moved = f32[4,1192,128]{2,1,0:T(8,128)S(1)} custom-call(f32[1152,512]{1,0:T(8,128)} %spectrum.1, f32[2,512]{1,0:T(2,128)} %wind_hbm.1, bf16[1152,1152]{1,0:T(8,128)(2,1)} %coupling.1, f32[32]{0:T(128)} %growth_hbm.1, f32[32]{0:T(128)} %dissipation_hbm.1, f32[32,32]{1,0:T(8,128)} %group_speed_hbm.1, f32[32,32]{1,0:T(8,128)} %refraction_hbm.1, ...), custom_call_target="tpu_custom_call" | custom-call | tf_op jit(solution)/shard_map/pallas_call | solution.py:598
  66.7 1.4 %shard_map.101 = f32[1152,512]{1,0:T(8,128)} custom-call(f32[4,1192,128]{2,1,0:T(8,128)S(1)} %shard_map.100.moved), custom_call_target="tpu_custom_call" | custom-call | tf_op jit(solution)/shard_map/pallas_call | solution.py:666
